TPU v7x, 32 devices: a whole 2x2x4 slice. The times are simulated.
32 devices in a mesh: depth: 4 (over x, core), gy: 4 (over z), gx: 2 (over y).
Axes of the slice: x: 2, y: 2, z: 4, core: 2. Of those that a mesh axis runs over, the one named last changes fastest.
Arguments:
- conserved_thermal_state: float32 [16, 2048, 512], P('depth', 'gy', 'gx'), may hold values from -2 to 30
- tier_depth_span: float32 [16], P('depth'), may hold values from 93.75 to 562.5
- water_tier_tally: int32 [2048, 512], P('gy', 'gx'), may hold values from 0 to 16
- regrid_sender_piece: int32 [4, 2, 2, 512], P('gy', 'gx'), may hold values from 0 to 1023
- regrid_receiver_piece: int32 [4, 2, 2, 512], P('gy', 'gx'), may hold values from 0 to 1023
- regrid_piece_coefficients: bfloat16 [4, 2, 2, 512, 16, 128], P('gy', 'gx'), may hold values from -0.5 to 0.5
- baseline_means: float32 [4, 512, 256], P('depth', 'gy', 'gx'), may hold values from 5 to 25
Outputs:
- anomaly: float32 [4, 512, 256], P('depth', 'gy', 'gx')
All inputs are finite; a program needn't handle non-finite values.
Results may differ from a plain program's by a relative error of at most 0.0003.
Values sent between devices are 32-bit elements; how exact they have to be, the bound alone decides.
A program may use at most 64 MiB of HBM per device.

v0:
```python
import jax
import jax.numpy as jnp
from jax import lax
from jax.sharding import PartitionSpec as P

SB = 128
TB = 16
SMOOTH = 2


cp_zero = 3991.86795711963
vol_zero = 0.00097
therm_one = 0.00017
therm_two = 5e-06
compress = 4.4e-06
bounds = (300.0, 700.0, 2000.0)
full_norm = 4000.0
smooth_nu = 0.2


def extended(cells, sides, width):
    for axis, dim in sides:
        count = lax.axis_size(axis)
        head = lax.slice_in_dim(cells, 0, width, axis=dim)
        tail = lax.slice_in_dim(cells, cells.shape[dim] - width, cells.shape[dim], axis=dim)
        cells = jnp.concatenate(
            [
                lax.ppermute(tail, axis, [(i, (i + 1) % count) for i in range(count)]),
                cells,
                lax.ppermute(head, axis, [((i + 1) % count, i) for i in range(count)]),
            ],
            axis=dim,
        )
    return cells


def prefix(value, axis, join, neutral):
    count, mine = (lax.axis_size(axis), lax.axis_index(axis))
    pieces = lax.all_gather(value, axis)
    running = jnp.full_like(value, 0) + jnp.asarray(neutral, value.dtype)

    def step(position, running):
        longer = join(running, pieces[position])
        return jnp.where(position < mine, longer, running)

    return lax.fori_loop(0, count - 1, step, running)


def tier_enthalpy_store(temp_layer, ocean_gauge_stress):
    expand = 1.0 + therm_one * temp_layer + therm_two * temp_layer * temp_layer
    volume = vol_zero * (expand - compress * ocean_gauge_stress)
    enthalpy = cp_zero * temp_layer + 10000.0 * vol_zero * (
        expand * ocean_gauge_stress - 0.5 * compress * ocean_gauge_stress * ocean_gauge_stress
    )
    return enthalpy / (volume * (cp_zero / vol_zero))


def depth_weights(level_tops, tier_depth_span):
    fractions = [
        jnp.clip(bound_depth - level_tops, 0.0, tier_depth_span) / bound_depth
        for bound_depth in bounds
    ]
    fractions.append(tier_depth_span / full_norm)
    return jnp.stack(fractions)


def combine_levels(weight_rows, heat_layers):
    return jnp.einsum("kl,lji->kji", weight_rows, heat_layers, precision=lax.Precision.HIGHEST)


def pad_tile(surface):
    padded = extended(surface, (("gy", 0), ("gx", 1)), 1)
    top_row = surface[-1]
    width = top_row.shape[0]
    gathered = lax.all_gather(top_row[None, :], "gx", axis=1, tiled=True)[0]
    mirrored = lax.dynamic_slice_in_dim(gathered[::-1], lax.axis_index("gx") * width, width, 0)
    row_index = lax.axis_index("gy")
    last_row = lax.axis_size("gy") - 1
    north_row = jnp.where(row_index == last_row, mirrored, padded[-1, 1:-1])
    south_row = jnp.where(row_index == 0, jnp.zeros_like(top_row), padded[0, 1:-1])
    return padded.at[-1, 1:-1].set(north_row).at[0, 1:-1].set(south_row)


def per_device(
    conserved_thermal_state,
    tier_depth_span,
    water_tier_tally,
    regrid_sender_piece,
    regrid_receiver_piece,
    regrid_piece_coefficients,
    baseline_means,
):
    slab_total = jnp.sum(tier_depth_span)
    offset = prefix(
        slab_total, "depth", lambda earlier, later: earlier + later, jnp.zeros((), jnp.float32)
    )
    level_tops = offset + jnp.concatenate(
        [jnp.zeros((1,), jnp.float32), jnp.cumsum(tier_depth_span)[:-1]]
    )
    ocean_gauge_stress = level_tops + 0.5 * tier_depth_span
    scaling_coefficients = depth_weights(level_tops, tier_depth_span)
    tier_floor_depth = lax.axis_index("depth") * conserved_thermal_state.shape[0]
    layer_sequence = []
    for tile_tier in range(conserved_thermal_state.shape[0]):
        water_tier_indicator = (tier_floor_depth + tile_tier < water_tier_tally).astype(jnp.float32)
        layer_sequence.append(
            tier_enthalpy_store(conserved_thermal_state[tile_tier], ocean_gauge_stress[tile_tier])
            * water_tier_indicator
        )
    heat_layers = jnp.stack(layer_sequence)
    level_terms = combine_levels(scaling_coefficients, heat_layers)
    summed = lax.psum_scatter(level_terms, "depth", scatter_dimension=0, tiled=True)
    surface = summed[0]
    wet_mask = (water_tier_tally > 0).astype(jnp.float32)
    wet_pad = pad_tile(wet_mask)
    for sweep_index in range(SMOOTH):
        padded = pad_tile(surface)
        net_flux = wet_pad[:-2, 1:-1] * (padded[:-2, 1:-1] - surface)
        net_flux = net_flux + wet_pad[2:, 1:-1] * (padded[2:, 1:-1] - surface)
        net_flux = net_flux + wet_pad[1:-1, :-2] * (padded[1:-1, :-2] - surface)
        net_flux = net_flux + wet_pad[1:-1, 2:] * (padded[1:-1, 2:] - surface)
        surface = surface + smooth_nu * wet_mask * net_flux
    groups = regrid_sender_piece.shape[2]
    blocks = surface.reshape(-1, SB)
    picked = jnp.take(blocks, regrid_sender_piece.reshape(-1), axis=0)
    weight_blocks = regrid_piece_coefficients.reshape(-1, TB, SB)
    contrib = jnp.einsum(
        "ptq,pq->pt", weight_blocks.astype(jnp.float32), picked, precision=lax.Precision.HIGHEST
    )
    targets = regrid_receiver_piece.reshape(groups, -1).astype(jnp.float32)
    received, recv_targets = (
        lax.all_to_all(contrib.reshape(groups, -1), "gx", split_axis=0, concat_axis=0, tiled=True),
        lax.all_to_all(targets, "gx", split_axis=0, concat_axis=0, tiled=True),
    )
    target_rows = baseline_means.shape[1]
    target_cols = baseline_means.shape[2]
    target_blocks = target_rows * target_cols // TB
    target_ids = recv_targets.reshape(-1).astype(jnp.int32)
    remapped = jax.ops.segment_sum(received.reshape(-1, TB), target_ids, num_segments=target_blocks)
    remapped = remapped.reshape(target_rows, target_cols)
    return (remapped - baseline_means[0])[None]


def solution(mesh):
    return jax.shard_map(
        per_device,
        mesh=mesh,
        in_specs=(
            P("depth", "gy", "gx"),
            P("depth"),
            P("gy", "gx"),
            P("gy", "gx", None, None),
            P("gy", "gx", None, None),
            P("gy", "gx", None, None, None, None),
            P("depth", "gy", "gx"),
        ),
        out_specs=P("depth", "gy", "gx"),
        check_vma=False,
    )
```

profile of v0, /device:TPU:0, one launch (start us, length us, event | category | flops | bytes accessed | tf_op | source)
XLA Modules:
  0.0 163.7 jit_solution(5383594202073741934)
XLA Ops:
  6.5 1.3 reduce_sum.9
  7.8 1.3 dynamic-slice.43
  9.1 1.4 dynamic-update-slice.12
  10.6 8.3 %all-reduce = f32[4]{0:T(128)S(1)} all-reduce(f32[4]{0:T(128)S(1)} %dynamic-update-slice.12), channel_id=1, replica_groups=mesh['depth'=4,'gy'=4,'gx'=2] {'depth'}, use_global_device_ids=true, to_apply=%add | all-reduce | flops 4 | bytes 32
  18.9 3.7 %while.19 = (s32[]{:T(128)}, f32[]{:T(128)}, s32[]{:T(128)}, f32[4]{0:T(128)S(1)}, s32[]{:T(128)}) while((s32[]{:T(128)}, f32[]{:T(128)}, s32[]{:T(128)}, f32[4]{0:T(128)S(1)}, s32[]{:T(128)}) %tuple.70), condition=%wide.region_2.3_spmd, body=%wide.region_1.2_spmd.sunk | while | flops 5 | bytes 107 | solution.py:46
  18.9 0.6 dynamic_slice.23
  20.1 0.6 dynamic_slice.23
  21.4 0.6 dynamic_slice.23
  22.6 0.8 reduce-window.4
  23.4 0.7 multiply_bitcast_fusion.3
  24.2 0.7 multiply_bitcast_fusion.2
  24.8 0.6 fusion.64
  32.2 4.2 %fusion.45 = (f32[1,512,256]{2,1,0:T(8,128)S(1)}, f32[1,512,256]{2,1,0:T(8,128)S(1)}, f32[512,256]{1,0:T(8,128)S(1)}) fusion(f32[4,512,256]{2,1,0:T(8,128)} %param.21, s32[512,256]{1,0:T(8,128)} %param.23, f32[]{:T(128)S(6)} %mul.204, f32[]{:T(128)S(6)} %mul.202, f32[]{:T(128)} %bitcast.13, s32[]{:T(128)S(6)} %mul.193, f32[]{:T(128)S(6)} %mul.216, ...), kind=kLoop, calls=%fused_computation.75 | loop fusion | flops 5898240 | bytes 3670064 | tf_op jit(solution)/shard_map/stack | solution.py:110
  36.4 0.5 copy.17
  36.9 0.5 copy.18
  37.5 0.4 stack.38
  38.5 1.9 %fusion.35 = f32[1,512,256]{2,1,0:T(8,128)S(1)} fusion(f32[4,512,256]{2,1,0:T(8,128)} %param.21, s32[512,256]{1,0:T(8,128)S(1)} %copy-done.1, f32[]{:T(128)S(6)} %mul.228, f32[]{:T(128)S(6)} %mul.226, f32[]{:T(128)} %bitcast.19, s32[]{:T(128)S(6)} %add.160), kind=kLoop, calls=%fused_computation.61 | loop fusion | flops 1966080 | bytes 1572880 | tf_op jit(solution)/shard_map/stack | solution.py:110
  40.4 0.5 copy.19
  41.0 5.2 %fusion = f32[4,512,256]{2,0,1:T(4,128)S(1)} fusion(f32[1,512,256]{2,0,1:T(1,128)S(1)} %stack.38, f32[1,512,256]{2,0,1:T(1,128)S(1)} %copy.19, f32[1,512,256]{2,0,1:T(1,128)S(1)} %copy.18, f32[1,512,256]{2,0,1:T(1,128)S(1)} %copy.17, f32[1,4]{1,0:T(1,128)S(1)} %get-tuple-element.190, f32[1,4]{1,0:T(1,128)S(1)} %get-tuple-element.186, ...), kind=kOutput, calls=%fused_computation.2 | convolution fusion | flops 26738736 | bytes 4194368 | tf_op jit(solution)/shard_map/kl,lji->kji/dot_general | solution.py:68
  46.2 1.7 %copy.20 = f32[4,512,256]{2,1,0:T(8,128)} copy(f32[4,512,256]{2,0,1:T(4,128)S(1)} %fusion) | data formatting | bytes 4194304 | tf_op jit(solution)/shard_map/kl,lji->kji/dot_general | solution.py:68
  48.1 1.6 %collective-permute-start = (f32[1,256]{1,0:T(1,128)S(1)}, f32[1,256]{1,0:T(1,128)S(1)}, u32[]{:S(2)}, u32[]{:S(2)}) collective-permute-start(f32[1,256]{1,0:T(1,128)S(1)} %get-tuple-element.180), channel_id=1, source_target_pairs={{0,2},{2,4},{4,6},{6,0},{1,3},{3,5},{5,7},{7,1},{8,10},{10,12},{12... | collective-permute-start | bytes 3080 | tf_op jit(solution)/shard_map/ppermute | solution.py:28
  49.7 2.2 %collective-permute-start.1 = (f32[1,256]{1,0:T(1,128)S(1)}, f32[1,256]{1,0:T(1,128)S(1)}, u32[]{:S(2)}, u32[]{:S(2)}) collective-permute-start(f32[1,256]{1,0:T(1,128)S(1)} %get-tuple-element.181), channel_id=1, source_target_pairs={{2,0},{4,2},{6,4},{0,6},{3,1},{5,3},{7,5},{1,7},{10,8},{12,10},{14... | collective-permute-start | bytes 3080 | tf_op jit(solution)/shard_map/ppermute | solution.py:30
  52.0 0.6 copy.28
  52.6 3.2 %all-to-all-start = ((f32[2,1,512]{2,1,0:T(1,128)}), f32[2,1,512]{2,1,0:T(1,128)S(1)}, u32[]{:S(2)}, u32[]{:S(2)}) async-start(f32[2,1,512]{2,1,0:T(1,128)} %bitcast.132), calls=%async_computation | async-start | bytes 8192 | tf_op jit(solution)/shard_map/all_to_all | solution.py:133
  55.8 0.6 fusion.63
  56.4 4.2 %all_gather.17 = f32[1,512]{1,0:T(1,128)S(1)} all-gather(f32[1,256]{1,0:T(1,128)S(1)} %get-tuple-element.180), channel_id=1, replica_groups=mesh['depth'=4,'gy'=4,'gx'=2] {'gx'}, dimensions={1}, use_global_device_ids=true | all-gather | bytes 3072 | tf_op jit(solution)/shard_map/all_gather | solution.py:75
  60.9 2.0 %collective-permute-start.2 = (f32[514,1]{1,0:T(8,128)S(1)}, f32[514,1]{1,0:T(8,128)S(1)}, u32[]{:S(2)}, u32[]{:S(2)}) collective-permute-start(f32[514,1]{1,0:T(8,128)S(1)} %get-tuple-element.174), channel_id=1, source_target_pairs={{0,1},{1,0},{2,3},{3,2},{4,5},{5,4},{6,7},{7,6},{8,9},{9,8},{10,11... | collective-permute-start | bytes 6176 | tf_op jit(solution)/shard_map/ppermute | solution.py:28
  63.1 6.3 %collective-permute-done.2 = f32[514,1]{1,0:T(8,128)S(1)} collective-permute-done((f32[514,1]{1,0:T(8,128)S(1)}, f32[514,1]{1,0:T(8,128)S(1)}, u32[]{:S(2)}, u32[]{:S(2)}) %collective-permute-start.2) | collective-permute-done | bytes 2088 | tf_op jit(solution)/shard_map/ppermute | solution.py:28
  69.4 2.9 %collective-permute-done.3 = f32[514,1]{1,0:T(8,128)S(1)} collective-permute-done((f32[514,1]{1,0:T(8,128)S(1)}, f32[514,1]{1,0:T(8,128)S(1)}, u32[]{:S(2)}, u32[]{:S(2)}) %collective-permute-start.3) | collective-permute-done | bytes 2088 | tf_op jit(solution)/shard_map/ppermute | solution.py:30
  72.3 0.4 pad_maximum_fusion
  72.6 7.3 %reduce-scatter.2.cloned.1.call-done = f32[1,512,256]{2,1,0:T(8,128)} async-done(((f32[4,512,256]{2,1,0:T(8,128)}), f32[1,512,256]{2,1,0:T(8,128)}) %reduce-scatter.2.cloned.1.call-update) | async-done | bytes 524304 | tf_op jit(solution)/shard_map/reduce_scatter | solution.py:112
  79.9 0.8 fusion.62
  80.7 3.3 %collective-permute-start.5 = (f32[1,256]{1,0:T(1,128)S(1)}, f32[1,256]{1,0:T(1,128)S(1)}, u32[]{:S(2)}, u32[]{:S(2)}) collective-permute-start(f32[1,256]{1,0:T(1,128)S(1)} %get-tuple-element.184), channel_id=1, source_target_pairs={{2,0},{4,2},{6,4},{0,6},{3,1},{5,3},{7,5},{1,7},{10,8},{12,10},{14... | collective-permute-start | bytes 3080 | tf_op jit(solution)/shard_map/ppermute | solution.py:30
  84.0 0.3 scatter.20
  84.3 1.7 %scatter.21 = f32[514,258]{1,0:T(8,128)S(1)} dynamic-update-slice(f32[514,258]{1,0:T(8,128)S(1)} %scatter.20, f32[1,256]{1,0:T(1,128)S(1)} %broadcast_select_fusion.3, s32[]{:T(128)} %bitcast.27, s32[]{:T(128)} %bitcast.28) | dynamic-update-slice | bytes 2052 | tf_op jit(solution)/shard_map/scatter | solution.py:81
  85.9 4.2 %all-gather = f32[1,1,512]{2,1,0:T(1,128)S(1)} all-gather(f32[1,1,256]{2,1,0:T(1,128)S(1)} %get-tuple-element.182), channel_id=2, replica_groups=mesh['depth'=4,'gy'=4,'gx'=2] {'gx'}, dimensions={2}, use_global_device_ids=true | all-gather | bytes 3072 | tf_op jit(solution)/shard_map/all_gather | solution.py:75
  90.3 1.1 pad_maximum_fusion.4
  91.5 1.5 collective-permute-start.6
  93.0 0.6 collective-permute-start.7
  93.7 7.2 %collective-permute-done.6 = f32[514,1]{1,0:T(8,128)S(1)} collective-permute-done((f32[514,1]{1,0:T(8,128)S(1)}, f32[514,1]{1,0:T(8,128)S(1)}, u32[]{:S(2)}, u32[]{:S(2)}) %collective-permute-start.6) | collective-permute-done | bytes 2088 | tf_op jit(solution)/shard_map/ppermute | solution.py:28
  100.9 3.4 %collective-permute-done.7 = f32[514,1]{1,0:T(8,128)S(1)} collective-permute-done((f32[514,1]{1,0:T(8,128)S(1)}, f32[514,1]{1,0:T(8,128)S(1)}, u32[]{:S(2)}, u32[]{:S(2)}) %collective-permute-start.7) | collective-permute-done | bytes 2088 | tf_op jit(solution)/shard_map/ppermute | solution.py:30
  104.3 0.4 pad_maximum_fusion.1
  104.6 0.4 scatter.24
  105.0 1.7 %scatter.25 = f32[514,258]{1,0:T(8,128)S(1)} dynamic-update-slice(f32[514,258]{1,0:T(8,128)S(1)} %scatter.24, f32[1,256]{1,0:T(1,128)S(1)} %broadcast_select_fusion.2, s32[]{:T(128)} %bitcast.27, s32[]{:T(128)} %bitcast.28) | dynamic-update-slice | bytes 2052 | tf_op jit(solution)/shard_map/scatter | solution.py:81
  106.7 0.9 fusion.8
  107.7 3.3 %collective-permute-start.9 = (f32[1,256]{1,0:T(1,128)S(1)}, f32[1,256]{1,0:T(1,128)S(1)}, u32[]{:S(2)}, u32[]{:S(2)}) collective-permute-start(f32[1,256]{1,0:T(1,128)S(1)} %get-tuple-element.179), channel_id=1, source_target_pairs={{2,0},{4,2},{6,4},{0,6},{3,1},{5,3},{7,5},{1,7},{10,8},{12,10},{14... | collective-permute-start | bytes 3080 | tf_op jit(solution)/shard_map/ppermute | solution.py:30
  111.0 4.4 %all_gather.19 = f32[1,512]{1,0:T(1,128)S(1)} all-gather(f32[1,256]{1,0:T(1,128)S(1)} %get-tuple-element.178), channel_id=1, replica_groups=mesh['depth'=4,'gy'=4,'gx'=2] {'gx'}, dimensions={1}, use_global_device_ids=true | all-gather | bytes 3072 | tf_op jit(solution)/shard_map/all_gather | solution.py:75
  115.5 0.8 collective-permute-done.8
  116.5 1.5 collective-permute-start.10
  118.0 0.6 collective-permute-start.11
  118.7 4.8 %collective-permute-done.10 = f32[514,1]{1,0:T(8,128)S(1)} collective-permute-done((f32[514,1]{1,0:T(8,128)S(1)}, f32[514,1]{1,0:T(8,128)S(1)}, u32[]{:S(2)}, u32[]{:S(2)}) %collective-permute-start.10) | collective-permute-done | bytes 2088 | tf_op jit(solution)/shard_map/ppermute | solution.py:28
  123.5 2.9 %collective-permute-done.11 = f32[514,1]{1,0:T(8,128)S(1)} collective-permute-done((f32[514,1]{1,0:T(8,128)S(1)}, f32[514,1]{1,0:T(8,128)S(1)}, u32[]{:S(2)}, u32[]{:S(2)}) %collective-permute-start.11) | collective-permute-done | bytes 2088 | tf_op jit(solution)/shard_map/ppermute | solution.py:30
  126.4 0.4 pad_maximum_fusion.2
  126.7 0.4 scatter.26
  127.1 1.7 %scatter.29 = f32[514,258]{1,0:T(8,128)S(1)} dynamic-update-slice(f32[514,258]{1,0:T(8,128)S(1)} %scatter.26, f32[1,256]{1,0:T(1,128)S(1)} %broadcast_select_fusion.1, s32[]{:T(128)} %bitcast.27, s32[]{:T(128)} %bitcast.28) | dynamic-update-slice | bytes 2052 | tf_op jit(solution)/shard_map/scatter | solution.py:81
  128.8 0.9 fusion.9
  129.8 2.8 %gather_fusion = f32[1024,128]{1,0:T(8,128)S(1)} fusion(f32[1024,128]{1,0:T(8,128)S(1)} %reshape.252, s32[1024]{0:T(1024)S(1)} %broadcast_clamp_fusion), kind=kCustom, calls=%fused_computation | custom fusion | bytes 1052672 | tf_op jit(solution)/shard_map/jit(_take)/gather | solution.py:125
  132.8 8.4 %fusion.65 = f32[1024,1,16]{2,1,0:T(1,128)S(1)} fusion(f32[1024,128,1]{1,2,0:T(1,128)S(1)} %bitcast.137, bf16[1024,16,128]{2,1,0:T(8,128)(2,1)} %bitcast.154), kind=kOutput, calls=%fused_computation.118 | convolution fusion | flops 25165824 | bytes 4784128 | tf_op jit(solution)/shard_map/ptq,pq->pt/dot_general | solution.py:127
  141.2 0.9 all_to_all.13
  142.0 3.3 %all-to-all-start.1 = ((f32[2,1,8192]{2,1,0:T(1,128)}), f32[2,1,8192]{2,1,0:T(1,128)S(1)}, u32[]{:S(2)}, u32[]{:S(2)}) async-start(f32[2,1,8192]{2,1,0:T(1,128)} %all_to_all.13), calls=%async_computation.2 | async-start | bytes 131072 | tf_op jit(solution)/shard_map/all_to_all | solution.py:132
  145.4 4.1 %all-to-all-done.1 = f32[2,1,8192]{2,1,0:T(1,128)S(1)} async-done(((f32[2,1,8192]{2,1,0:T(1,128)}), f32[2,1,8192]{2,1,0:T(1,128)S(1)}, u32[]{:S(2)}, u32[]{:S(2)}) %all-to-all-start.1) | async-done | bytes 65568 | tf_op jit(solution)/shard_map/all_to_all | solution.py:132
  149.7 0.2 reshape.269
  149.9 6.1 %scatter_custom_fusion = f32[1024,16]{1,0:T(8,128)S(1)} fusion(s32[1024]{0:T(1024)S(1)} %bitcast.149, f32[1024,16]{1,0:T(8,128)S(1)} %reshape.269, f32[]{:T(128)} %constant.206.clone.1), kind=kCustom, calls=%fused_computation.79 | custom fusion | flops 16384 | bytes 65540 | tf_op jit(solution)/shard_map/scatter-add | solution.py:139
  156.2 0.6 sub.112
  (52 shorter events, 1.9 us)
Async XLA Ops:
  6.5 73.3 %reduce-scatter.2.cloned.1.call-start = ((), (), s32[]{:S(2)}) async-start(), calls=%async_computation.3 | async-start | bytes 2621440 | tf_op jit(solution)/shard_map/reduce_scatter | solution.py:112
  36.4 2.1 %copy-start.1 = (s32[512,256]{1,0:T(8,128)S(1)}, s32[512,256]{1,0:T(8,128)}, u32[]{:S(2)}) copy-start(s32[512,256]{1,0:T(8,128)} %param.23) | copy-start | bytes 1572868
  47.9 4.0 %copy-start.4 = (s32[1,1,2,512]{3,2,1,0:T(2,128)S(1)}, s32[1,1,2,512]{3,2,1,0:T(2,128)}, u32[]{:S(2)}) copy-start(s32[1,1,2,512]{3,2,1,0:T(2,128)} %param.25) | copy-start | bytes 12292
  47.9 7.8 %copy-start.3 = (s32[1,1,2,512]{3,2,1,0:T(2,128)S(1)}, s32[1,1,2,512]{3,2,1,0:T(2,128)}, u32[]{:S(2)}) copy-start(s32[1,1,2,512]{3,2,1,0:T(2,128)} %param.24) | copy-start | bytes 12292
  48.1 12.7 %collective-permute-start = (f32[1,256]{1,0:T(1,128)S(1)}, f32[1,256]{1,0:T(1,128)S(1)}, u32[]{:S(2)}, u32[]{:S(2)}) collective-permute-start(f32[1,256]{1,0:T(1,128)S(1)} %get-tuple-element.180), channel_id=1, source_target_pairs={{0,2},{2,4},{4,6},{6,0},{1,3},{3,5},{5,7},{7,1},{8,10},{10,12},{12... | collective-permute-start | bytes 3080 | tf_op jit(solution)/shard_map/ppermute | solution.py:28
  49.7 11.0 %collective-permute-start.1 = (f32[1,256]{1,0:T(1,128)S(1)}, f32[1,256]{1,0:T(1,128)S(1)}, u32[]{:S(2)}, u32[]{:S(2)}) collective-permute-start(f32[1,256]{1,0:T(1,128)S(1)} %get-tuple-element.181), channel_id=1, source_target_pairs={{2,0},{4,2},{6,4},{0,6},{3,1},{5,3},{7,5},{1,7},{10,8},{12,10},{14... | collective-permute-start | bytes 3080 | tf_op jit(solution)/shard_map/ppermute | solution.py:30
  52.6 89.5 %all-to-all-start = ((f32[2,1,512]{2,1,0:T(1,128)}), f32[2,1,512]{2,1,0:T(1,128)S(1)}, u32[]{:S(2)}, u32[]{:S(2)}) async-start(f32[2,1,512]{2,1,0:T(1,128)} %bitcast.132), calls=%async_computation | async-start | bytes 8192 | tf_op jit(solution)/shard_map/all_to_all | solution.py:133
  60.9 8.5 %collective-permute-start.2 = (f32[514,1]{1,0:T(8,128)S(1)}, f32[514,1]{1,0:T(8,128)S(1)}, u32[]{:S(2)}, u32[]{:S(2)}) collective-permute-start(f32[514,1]{1,0:T(8,128)S(1)} %get-tuple-element.174), channel_id=1, source_target_pairs={{0,1},{1,0},{2,3},{3,2},{4,5},{5,4},{6,7},{7,6},{8,9},{9,8},{10,11... | collective-permute-start | bytes 6176 | tf_op jit(solution)/shard_map/ppermute | solution.py:28
  63.0 9.3 %collective-permute-start.3 = (f32[514,1]{1,0:T(8,128)S(1)}, f32[514,1]{1,0:T(8,128)S(1)}, u32[]{:S(2)}, u32[]{:S(2)}) collective-permute-start(f32[514,1]{1,0:T(8,128)S(1)} %get-tuple-element.175), channel_id=1, source_target_pairs={{1,0},{0,1},{3,2},{2,3},{5,4},{4,5},{7,6},{6,7},{9,8},{8,9},{11,10... | collective-permute-start | bytes 6176 | tf_op jit(solution)/shard_map/ppermute | solution.py:30
  79.9 24.4 %copy-start = (f32[1,512,256]{2,1,0:T(8,128)S(1)}, f32[1,512,256]{2,1,0:T(8,128)}, u32[]{:S(2)}) copy-start(f32[1,512,256]{2,1,0:T(8,128)} %reduce-scatter.2.cloned.1.call-done) | copy-start | bytes 1572868
  80.7 9.6 %collective-permute-start.5 = (f32[1,256]{1,0:T(1,128)S(1)}, f32[1,256]{1,0:T(1,128)S(1)}, u32[]{:S(2)}, u32[]{:S(2)}) collective-permute-start(f32[1,256]{1,0:T(1,128)S(1)} %get-tuple-element.184), channel_id=1, source_target_pairs={{2,0},{4,2},{6,4},{0,6},{3,1},{5,3},{7,5},{1,7},{10,8},{12,10},{14... | collective-permute-start | bytes 3080 | tf_op jit(solution)/shard_map/ppermute | solution.py:30
  84.0 6.3 %collective-permute-start.4 = (f32[1,256]{1,0:T(1,128)S(1)}, f32[1,256]{1,0:T(1,128)S(1)}, u32[]{:S(2)}, u32[]{:S(2)}) collective-permute-start(f32[1,256]{1,0:T(1,128)S(1)} %get-tuple-element.183), channel_id=1, source_target_pairs={{0,2},{2,4},{4,6},{6,0},{1,3},{3,5},{5,7},{7,1},{8,10},{10,12},{12... | collective-permute-start | bytes 3080 | tf_op jit(solution)/shard_map/ppermute | solution.py:28
  91.5 9.4 %collective-permute-start.6 = (f32[514,1]{1,0:T(8,128)S(1)}, f32[514,1]{1,0:T(8,128)S(1)}, u32[]{:S(2)}, u32[]{:S(2)}) collective-permute-start(f32[514,1]{1,0:T(8,128)S(1)} %get-tuple-element.176), channel_id=1, source_target_pairs={{0,1},{1,0},{2,3},{3,2},{4,5},{5,4},{6,7},{7,6},{8,9},{9,8},{10,11... | collective-permute-start | bytes 6176 | tf_op jit(solution)/shard_map/ppermute | solution.py:28
  93.0 11.2 %collective-permute-start.7 = (f32[514,1]{1,0:T(8,128)S(1)}, f32[514,1]{1,0:T(8,128)S(1)}, u32[]{:S(2)}, u32[]{:S(2)}) collective-permute-start(f32[514,1]{1,0:T(8,128)S(1)} %get-tuple-element.177), channel_id=1, source_target_pairs={{1,0},{0,1},{3,2},{2,3},{5,4},{4,5},{7,6},{6,7},{9,8},{8,9},{11,10... | collective-permute-start | bytes 6176 | tf_op jit(solution)/shard_map/ppermute | solution.py:30
  107.7 7.8 %collective-permute-start.9 = (f32[1,256]{1,0:T(1,128)S(1)}, f32[1,256]{1,0:T(1,128)S(1)}, u32[]{:S(2)}, u32[]{:S(2)}) collective-permute-start(f32[1,256]{1,0:T(1,128)S(1)} %get-tuple-element.179), channel_id=1, source_target_pairs={{2,0},{4,2},{6,4},{0,6},{3,1},{5,3},{7,5},{1,7},{10,8},{12,10},{14... | collective-permute-start | bytes 3080 | tf_op jit(solution)/shard_map/ppermute | solution.py:30
  111.0 5.4 %collective-permute-start.8 = (f32[1,256]{1,0:T(1,128)S(1)}, f32[1,256]{1,0:T(1,128)S(1)}, u32[]{:S(2)}, u32[]{:S(2)}) collective-permute-start(f32[1,256]{1,0:T(1,128)S(1)} %get-tuple-element.178), channel_id=1, source_target_pairs={{0,2},{2,4},{4,6},{6,0},{1,3},{3,5},{5,7},{7,1},{8,10},{10,12},{12... | collective-permute-start | bytes 3080 | tf_op jit(solution)/shard_map/ppermute | solution.py:28
  116.5 7.0 %collective-permute-start.10 = (f32[514,1]{1,0:T(8,128)S(1)}, f32[514,1]{1,0:T(8,128)S(1)}, u32[]{:S(2)}, u32[]{:S(2)}) collective-permute-start(f32[514,1]{1,0:T(8,128)S(1)} %get-tuple-element.172), channel_id=1, source_target_pairs={{0,1},{1,0},{2,3},{3,2},{4,5},{5,4},{6,7},{7,6},{8,9},{9,8},{10,11... | collective-permute-start | bytes 6176 | tf_op jit(solution)/shard_map/ppermute | solution.py:28
  118.0 8.3 %collective-permute-start.11 = (f32[514,1]{1,0:T(8,128)S(1)}, f32[514,1]{1,0:T(8,128)S(1)}, u32[]{:S(2)}, u32[]{:S(2)}) collective-permute-start(f32[514,1]{1,0:T(8,128)S(1)} %get-tuple-element.173), channel_id=1, source_target_pairs={{1,0},{0,1},{3,2},{2,3},{5,4},{4,5},{7,6},{6,7},{9,8},{8,9},{11,10... | collective-permute-start | bytes 6176 | tf_op jit(solution)/shard_map/ppermute | solution.py:30
  141.2 15.1 %copy-start.2 = (f32[1,128,128]{2,1,0:T(8,128)S(1)}, f32[1,128,128]{2,1,0:T(8,128)}, u32[]{:S(2)}) copy-start(f32[1,128,128]{2,1,0:T(8,128)} %param.27) | copy-start | bytes 196612
  142.0 7.4 %all-to-all-start.1 = ((f32[2,1,8192]{2,1,0:T(1,128)}), f32[2,1,8192]{2,1,0:T(1,128)S(1)}, u32[]{:S(2)}, u32[]{:S(2)}) async-start(f32[2,1,8192]{2,1,0:T(1,128)} %all_to_all.13), calls=%async_computation.2 | async-start | bytes 131072 | tf_op jit(solution)/shard_map/all_to_all | solution.py:132
Sparse Core Ops, SparseCore 0:
  48.1 31.7 reduce-scatter.1
where the time goes:
time: 164 us
  waiting for transfers between devices  39.6 us (24%)
  starting transfers between devices  23.3 us (14%)
  local copies, waits for them, and re-layouts  21.7 us (13%)
  other arithmetic  21.2 us (13%)
  blocking collectives  21.2 us (13%)
  between operations  21.1 us (13%)
  matrix products  13.6 us (8%)
  loops' own time  1.94 us (1%)
    ppermute x6, waiting for transfers between devices, extended(): lax.ppermute(tail, axis, [(i, (i + 1) % count) for i in range(count)])  19.2 us
    all_gather x3, blocking collectives, pad_tile(): gathered = lax.all_gather(top_row[None, :], 'gx', axis=1, tiled=True)[0]  12.9 us
    ppermute x6, starting transfers between devices, extended(): lax.ppermute(head, axis, [((i + 1) % count, i) for i in range(count)])  10.1 us
    ppermute x6, waiting for transfers between devices, extended(): lax.ppermute(head, axis, [((i + 1) % count, i) for i in range(count)])  9.09 us
    dot_general x1, matrix products, per_device(): jnp.einsum('ptq,pq->pt', weight_blocks.astype(jnp.float32), picked, preci...  8.36 us
    unnamed x1, blocking collectives  8.31 us
    reduce_scatter x1, waiting for transfers between devices, per_device(): lax.psum_scatter(level_terms, 'depth', scatter_dimension=0, tiled=True)  7.25 us
    ppermute x6, starting transfers between devices, extended(): lax.ppermute(tail, axis, [(i, (i + 1) % count) for i in range(count)])  6.75 us
  transfers between devices with their start and end apart: 15, of which 9 were waited for; matrix products, arithmetic and copies ran while one was open for 15% of the time, Pallas kernels for 0%

commit v1 on v0

v1 whole, which is shorter than its diff:
```python
import functools

import jax
import jax.numpy as jnp
from jax import lax
from jax.experimental import pallas as pl
from jax.experimental.pallas import tpu as pltpu
from jax.sharding import PartitionSpec as P

SB = 128
TB = 16

cp_zero = 3991.86795711963
vol_zero = 0.00097
therm_one = 0.00017
therm_two = 5e-06
compress = 4.4e-06
bounds = (300.0, 700.0, 2000.0)
full_norm = 4000.0
smooth_nu = 0.2

MESH = pl.DeviceIdType.MESH
F32 = jnp.float32
BF16 = jnp.bfloat16
PAD = 8


def lanes(shape):
    return lax.broadcasted_iota(jnp.int32, shape, len(shape) - 1)


def sublanes(shape):
    return lax.broadcasted_iota(jnp.int32, shape, len(shape) - 2)


def split_two(x):
    hi = x.astype(BF16)
    lo = (x - hi.astype(F32)).astype(BF16)
    return hi, lo


def kernel(
    nd, ny, nx, cap, unroll,
    span_s, pick_s, temp_h, tally_v, tgt_v, coef_h, base_v,
    out_v,
    temp_v, coef_v, fa, fb, acoef, store, pack, pin, pint,
    col_out, col_in, row_out, row_in, th_out, th_in, prm,
    vout, vin, tslot, onehot, eexp,
    temp_sem, coef_sem, col_ss, col_rs, row_ss, row_rs, th_ss, th_rs, tg_ss, tg_rs, v_ss, v_rs,
):
    d, y, b = lax.axis_index("depth"), lax.axis_index("gy"), lax.axis_index("gx")
    nl, rows, cols = temp_v.shape
    chunks = temp_sem.shape[0]
    crow = rows // chunks
    last = ny - 1
    east, west = lax.rem(b + 1, nx), lax.rem(b + nx - 1, nx)
    mirror = nx - 1 - b

    temp_copies = []
    for q in range(chunks):
        span = pl.ds(q * crow, crow)
        copy = pltpu.make_async_copy(temp_h.at[:, span, :], temp_v.at[:, span, :], temp_sem.at[q])
        copy.start()
        temp_copies.append(copy)
    coef_copies = []
    for j in list(range(1, nx)) + [0]:
        c = lax.rem(b + j, nx)
        copy = pltpu.make_async_copy(coef_h.at[c], coef_v.at[j], coef_sem.at[j])
        copy.start()
        coef_copies.append(copy)

    row_in[...] = jnp.zeros(row_in.shape, F32)

    barrier = pltpu.get_barrier_semaphore()
    peers = [(i, j) for i in range(nd) for j in range(nx) if (i, j) != (0, 0)]
    for i, j in peers:
        pl.semaphore_signal(
            barrier, inc=1, device_id=(lax.rem(d + i, nd), y, lax.rem(b + j, nx)), device_id_type=MESH
        )

    @pl.when(y > 0)
    def _():
        pl.semaphore_signal(barrier, inc=1, device_id=(d, y - 1, b), device_id_type=MESH)

    @pl.when(y < last)
    def _():
        pl.semaphore_signal(barrier, inc=1, device_id=(d, y + 1, b), device_id_type=MESH)

    thick = [span_s[l] for l in range(nl)]
    total = thick[0]
    for l in range(1, nl):
        total = total + thick[l]
    th_out[...] = jnp.full(th_out.shape, total, F32)
    zero_rows = jnp.zeros((PAD, cols), F32)
    for m in range(5):
        for buf in (fa, fb):
            buf[m, 0:PAD, :] = zero_rows
            buf[m, PAD + rows:, :] = zero_rows
    pint[...] = jnp.zeros(pint.shape, F32)
    col_out[...] = jnp.zeros(col_out.shape, F32)
    row_out[...] = jnp.zeros(row_out.shape, F32)

    inner = jnp.logical_and(y > 0, y < last)

    @pl.when(inner)
    def _():
        pl.semaphore_wait(barrier, len(peers) + 2)

    @pl.when(jnp.logical_not(inner))
    def _():
        pl.semaphore_wait(barrier, len(peers) + 1)

    th_copies = []
    for i in range(1, nd):
        copy = pltpu.make_async_remote_copy(
            th_out, th_in.at[i], th_ss.at[i], th_rs.at[i], (lax.rem(d + i, nd), y, b), MESH
        )
        copy.start()
        th_copies.append(copy)
    tg_copies = []
    for j in range(1, nx):
        c = lax.rem(b + j, nx)
        copy = pltpu.make_async_remote_copy(
            tgt_v.at[c], tslot.at[j], tg_ss.at[j], tg_rs.at[j], (d, y, c), MESH
        )
        copy.start()
        tg_copies.append(copy)
    tslot[0] = tgt_v[b]

    top = jnp.zeros((8, 128), F32)
    for i in range(1, nd):
        th_copies[i - 1].wait()
        top = top + jnp.where(d >= i, th_in[i], 0.0)
    alpha = 10000.0 * vol_zero / cp_zero
    for l in range(nl):
        press = top + 0.5 * thick[l]
        prm[l, 0] = alpha * press
        prm[l, 1] = (0.5 * alpha * compress) * press * press
        prm[l, 2] = compress * press
        for k, depth in enumerate(bounds):
            prm[l, 3 + k] = jnp.clip(depth - top, 0.0, thick[l]) / depth
        prm[l, 6] = jnp.full((8, 128), thick[l] / full_norm, F32)
        top = top + thick[l]

    lane = lanes((8, 128))
    first_lane, last_lane = lane == 0, lane == 127
    row_tile = lambda r: pl.multiple_of(r * 8, 8)

    def pack_edges(pairs):
        packed = jnp.zeros((8, 128), F32)
        for m, (left, right) in enumerate(pairs):
            edge = jnp.where(first_lane, left, right)
            packed = jnp.where((lane >> 1) == m, pltpu.roll(edge, 2 * m + 1, 1), packed)
        return packed

    def heat_rows(r, carry):
        base = row_tile(r)
        pairs = [[None, None] for _ in range(5)]
        for h in range(2):
            here = (pl.ds(base, 8), slice(128 * h, 128 * h + 128))
            tally = tally_v[here]
            sums = [None] * 4
            for l in range(nl):
                t = temp_v[(l,) + here]
                expand = 1.0 + t * (therm_one + therm_two * t)
                heat = (t + prm[l, 0] * expand - prm[l, 1]) / (expand - prm[l, 2])
                heat = jnp.where(d * nl + l < tally, heat, 0.0)
                for k in range(4):
                    term = prm[l, 3 + k] * heat
                    sums[k] = term if l == 0 else sums[k] + term
            sums.append(jnp.where(tally > 0, 1.0, 0.0))
            for m in range(5):
                fa[m, pl.ds(base + PAD, 8), 128 * h:128 * h + 128] = sums[m]
                pairs[m][h] = sums[m]
        pack[pl.ds(base, 8), :] = pack_edges(pairs)
        return carry

    for q in range(chunks):
        temp_copies[q].wait()
        lax.fori_loop(q * crow // 8, (q + 1) * crow // 8, heat_rows, 0, unroll=2)

    def send_edges(e, buf):
        for q in range(rows // 128):
            span = slice(128 * q, 128 * q + 128)
            turned = pack[span, :].T
            for m in range(5):
                col_out[e, 0, m:m + 1, span] = turned[2 * m:2 * m + 1]
                col_out[e, 1, m:m + 1, span] = turned[2 * m + 1:2 * m + 2]
        for m in range(5):
            src = fa if m == 4 else buf
            row_out[e, 0, m:m + 1, :] = src[m, PAD + rows - 1:PAD + rows, :]
            row_out[e, 1, m:m + 1, :] = src[m, PAD:PAD + 1, :]
        to_east = pltpu.make_async_remote_copy(
            col_out.at[e, 0], col_in.at[e, 0], col_ss.at[e, 0], col_rs.at[e, 0], (d, y, east), MESH
        )
        to_west = pltpu.make_async_remote_copy(
            col_out.at[e, 1], col_in.at[e, 1], col_ss.at[e, 1], col_rs.at[e, 1], (d, y, west), MESH
        )
        to_east.start()
        to_west.start()

        @pl.when(y < last)
        def _():
            pltpu.make_async_remote_copy(
                row_out.at[e, 0], row_in.at[e, 1], row_ss.at[e, 0], row_rs.at[e, 1], (d, y + 1, b), MESH
            ).start()

        @pl.when(y == last)
        def _():
            pltpu.make_async_remote_copy(
                row_out.at[e, 0], row_in.at[e, 0], row_ss.at[e, 0], row_rs.at[e, 0], (d, y, mirror), MESH
            ).start()

        @pl.when(y > 0)
        def _():
            pltpu.make_async_remote_copy(
                row_out.at[e, 1], row_in.at[e, 0], row_ss.at[e, 1], row_rs.at[e, 0], (d, y - 1, b), MESH
            ).start()

        return to_east, to_west

    def receive_edges(e, copies):
        for copy in copies:
            copy.wait()
        north = pltpu.make_async_remote_copy(
            row_out.at[e, 0], row_in.at[e, 0], row_ss.at[e, 0], row_rs.at[e, 0], (d, y, mirror), MESH
        )
        north.wait_send()
        north.wait_recv()

        @pl.when(y > 0)
        def _():
            south = pltpu.make_async_remote_copy(
                row_out.at[e, 1], row_in.at[e, 1], row_ss.at[e, 1], row_rs.at[e, 1], (d, y - 1, b), MESH
            )
            south.wait_send()
            south.wait_recv()

        @pl.when(y == last)
        def _():
            shape = (cols, cols)
            flip = jnp.where(lanes(shape) + sublanes(shape) == cols - 1, 1.0, 0.0)
            row_in[e, 0] = jnp.dot(
                row_in[e, 0], flip, precision=lax.Precision.HIGHEST, preferred_element_type=F32
            )

        for m in range(5):
            pint[2 * m:2 * m + 1, :] = col_in[e, 1, m:m + 1, :]
            pint[2 * m + 1:2 * m + 2, :] = col_in[e, 0, m:m + 1, :]
        for q in range(rows // 128):
            span = slice(128 * q, 128 * q + 128)
            pin[span, :] = pint[:, span].T

    tall = 32

    def neighbours(buf, m, base):
        wide = lanes((tall, cols))
        around = buf[m, pl.ds(base, tall + 2 * PAD), :]
        here = around[PAD:PAD + tall]
        up = around[PAD + 1:PAD + 1 + tall]
        down = around[PAD - 1:PAD - 1 + tall]
        left = jnp.where(wide == 0, 0.0, pltpu.roll(here, 1, 1))
        right = jnp.where(wide == cols - 1, 0.0, pltpu.roll(here, cols - 1, 1))
        return here, (up + down) + (left + right)

    def sweep(src, dst, build):
        def body(r, carry):
            base = pl.multiple_of(r * tall, tall)
            if build:
                wet, count = neighbours(fa, 4, base)
                keep = 1.0 - smooth_nu * count
                acoef[pl.ds(base, tall), :] = keep
            else:
                wet = fa[4, pl.ds(base + PAD, tall), :]
                keep = acoef[pl.ds(base, tall), :]
            gain = smooth_nu * wet
            for k in range(4):
                here, around = neighbours(src, k, base)
                dst[k, pl.ds(base + PAD, tall), :] = keep * here + gain * around
            return carry

        lax.fori_loop(0, rows // tall, body, 0)

    def fix_rows(e, src, dst):
        for side, row in ((0, PAD + rows - 1), (1, PAD)):
            wet_edge = row_in[e, side, 4:5, :]
            gain = smooth_nu * fa[4, row:row + 1, :]
            for k in range(4):
                more = gain * (row_in[e, side, k:k + 1, :] - wet_edge * src[k, row:row + 1, :])
                dst[k, row:row + 1, :] = dst[k, row:row + 1, :] + more

    def fix_columns(src, dst, base):
        here = pl.ds(base + PAD, 8)
        edges = pin[pl.ds(base, 8), :]
        wet_edge = pltpu.roll(edges, 128 - 9, 1)
        fixed = []
        for k in range(4):
            field_edge = pltpu.roll(edges, 128 - (2 * k + 1), 1)
            pair = []
            for h, mask in ((0, first_lane), (1, last_lane)):
                at = (k, here, slice(128 * h, 128 * h + 128))
                gain = smooth_nu * fa[(4,) + at[1:]]
                more = gain * (field_edge - wet_edge * src[at])
                pair.append(dst[at] + jnp.where(mask, more, 0.0))
            fixed.append(pair)
        return fixed

    edges = send_edges(0, fa)
    sweep(fa, fb, True)
    receive_edges(0, edges)
    fix_rows(0, fa, fb)

    def fix_first(r, carry):
        base = row_tile(r)
        fixed = fix_columns(fa, fb, base)
        for k in range(4):
            for h in range(2):
                fb[k, pl.ds(base + PAD, 8), 128 * h:128 * h + 128] = fixed[k][h]
        wet = [fa[4, pl.ds(base + PAD, 8), 128 * h:128 * h + 128] for h in range(2)]
        pack[pl.ds(base, 8), :] = pack_edges(fixed + [wet])
        return carry

    lax.fori_loop(0, rows // 8, fix_first, 0, unroll=2)
    edges = send_edges(1, fb)
    sweep(fb, fa, False)
    receive_edges(1, edges)
    fix_rows(1, fb, fa)

    def fix_second(r, carry):
        base = row_tile(r)
        fixed = fix_columns(fb, fa, base)
        for h in range(2):
            parts = []
            for k in range(4):
                parts.append(fixed[k][h].astype(BF16).astype(F32))
            for k in range(4):
                parts.append(fixed[k][h] - parts[k])
            block = jnp.swapaxes(jnp.stack(parts), 0, 1)
            store[pl.ds(h * rows + base, 8)] = block
        return carry

    lax.fori_loop(0, rows // 8, fix_second, 0, unroll=2)

    group = lane >> 4
    v_copies = []
    for j in list(range(1, nx)) + [0]:
        c = lax.rem(b + j, nx)
        coef_copies[(j - 1) % nx].wait()

        def remap(u, carry, c=c, j=j):
            for s in range(unroll):
                g = u * unroll + s
                picked = []
                for p in range(16):
                    at = pick_s[c * cap + g * 16 + p]
                    picked.append(store[(at & 1) * rows + (at >> 1)])
                block = jnp.concatenate(picked, axis=0).astype(BF16)
                weights = coef_v[j, pl.ds(pl.multiple_of(g * 256, 256), 256), :]
                prod = lax.dot_general(
                    block, weights, (((1,), (1,)), ((), ())), preferred_element_type=F32
                )
                for half in range(2):
                    tight = jnp.zeros((8, 128), F32)
                    for p in range(8):
                        row = (half * 8 + p) * 8
                        tight = jnp.where(
                            group == p, prod[row:row + 8, 128 * half:128 * half + 128], tight
                        )
                    tight = tight[0:4] + tight[4:8]
                    for k in range(4):
                        vout[lax.rem(k - d + nd, nd), j, pl.ds(g * 2 + half, 1), :] = tight[k:k + 1]
            return carry

        lax.fori_loop(0, cap // (16 * unroll), remap, 0)
        for i in range(nd):
            if (i, j) != (0, 0):
                copy = pltpu.make_async_remote_copy(
                    vout.at[i, j], vin.at[i, j], v_ss.at[i, j], v_rs.at[i, j],
                    (lax.rem(d + i, nd), y, c), MESH,
                )
                copy.start()
                v_copies.append(copy)

    for copy in tg_copies:
        copy.wait()
    tr = out_v.shape[0]
    for j in range(nx):
        ids = tslot[j]
        for q in range(8):
            shape = (tr, cap)
            wanted = sublanes(shape) * 8 + q
            onehot[q * tr:(q + 1) * tr, j * cap:(j + 1) * cap] = jnp.where(
                wanted == ids, 1.0, 0.0
            ).astype(BF16)
    for copy in v_copies:
        copy.wait()
    gr = cap // 8
    own_group = (lanes((gr, 8, 128)) >> 4) == lax.broadcasted_iota(jnp.int32, (gr, 8, 128), 1)
    for j in range(nx):
        summed = vout[0, 0] if j == 0 else vin[0, j]
        for i in range(1, nd):
            summed = summed + vin[i, j]
        spread = jnp.where(own_group, summed[:, None, :], 0.0).reshape(cap, 128)
        hi, lo = split_two(spread)
        eexp[j * cap:(j + 1) * cap, 0:128] = hi
        eexp[j * cap:(j + 1) * cap, 128:256] = lo
    both = jnp.dot(onehot[...], eexp[...], preferred_element_type=F32)
    hi, lo = split_two(both[:, 0:128] + both[:, 128:256])
    shape = (128, 128)
    tile16 = jnp.where((lanes(shape) & 15) == (sublanes(shape) & 15), 1.0, 0.0).astype(BF16)
    spread = jnp.dot(hi, tile16, preferred_element_type=F32) + jnp.dot(
        lo, tile16, preferred_element_type=F32
    )
    result = jnp.zeros((tr, 128), F32)
    where_q = lanes((tr, 128)) >> 4
    for q in range(8):
        result = jnp.where(where_q == q, spread[q * tr:(q + 1) * tr], result)
    out_v[...] = result - base_v[...]


def per_device(sizes, temp, span, tally, sender, receiver, coef, base):
    nd, ny, nx = sizes
    nl, rows, cols = temp.shape
    cap = sender.shape[-1]
    unroll = min(8, cap // 16)
    blocks = rows * cols // SB
    vmem = pltpu.VMEM
    dma = pltpu.SemaphoreType.DMA
    any_spec = pl.BlockSpec(memory_space=pl.ANY)
    vspec = pl.BlockSpec(memory_space=vmem)
    sspec = pl.BlockSpec(memory_space=pltpu.SMEM)
    tr, tc = base.shape[1:]
    scratch = [
        vmem((nl, rows, cols), F32),
        vmem((nx, cap * TB, SB), BF16),
        vmem((5, rows + 2 * PAD, cols), F32),
        vmem((5, rows + 2 * PAD, cols), F32),
        vmem((rows, cols), F32),
        vmem((blocks, 8, SB), F32),
        vmem((rows, 128), F32),
        vmem((rows, 128), F32),
        vmem((128, rows), F32),
        vmem((2, 2, 8, rows), F32),
        vmem((2, 2, 8, rows), F32),
        vmem((2, 2, 8, cols), F32),
        vmem((2, 2, 8, cols), F32),
        vmem((8, 128), F32),
        vmem((nd, 8, 128), F32),
        vmem((nl, 7, 8, 128), F32),
        vmem((nd, nx, cap // 8, 128), F32),
        vmem((nd, nx, cap // 8, 128), F32),
        vmem((nx, 1, cap), jnp.int32),
        vmem((8 * tr, nx * cap), BF16),
        vmem((nx * cap, 256), BF16),
        dma((4,)),
        dma((nx,)),
        dma((2, 2)), dma((2, 2)),
        dma((2, 2)), dma((2, 2)),
        dma((nd,)), dma((nd,)),
        dma((nx,)), dma((nx,)),
        dma((nd, nx)), dma((nd, nx)),
    ]
    out = pl.pallas_call(
        functools.partial(kernel, nd, ny, nx, cap, unroll),
        out_shape=jax.ShapeDtypeStruct((tr, tc), F32),
        in_specs=[sspec, sspec, any_spec, vspec, vspec, any_spec, vspec],
        out_specs=vspec,
        scratch_shapes=scratch,
        compiler_params=pltpu.CompilerParams(
            collective_id=0, has_side_effects=True, vmem_limit_bytes=48 * 1024 * 1024
        ),
    )(
        span,
        sender.reshape(-1),
        temp,
        tally,
        receiver.reshape(nx, 1, cap),
        coef.reshape(nx, cap * TB, SB),
        base[0],
    )
    return out[None]


def solution(mesh):
    sizes = tuple(mesh.shape[a] for a in ("depth", "gy", "gx"))
    return jax.shard_map(
        functools.partial(per_device, sizes),
        mesh=mesh,
        in_specs=(
            P("depth", "gy", "gx"),
            P("depth"),
            P("gy", "gx"),
            P("gy", "gx", None, None),
            P("gy", "gx", None, None),
            P("gy", "gx", None, None, None, None),
            P("depth", "gy", "gx"),
        ),
        out_specs=P("depth", "gy", "gx"),
        check_vma=False,
    )
```

time: 164 us -> 41.2 us (0.25)
  waiting for transfers between devices: 39.6 us -> 0 us
  Pallas kernels: 0 us -> 34.8 us
  starting transfers between devices: 23.3 us -> 0 us
  other arithmetic: 21.2 us -> 0 us
  blocking collectives: 21.2 us -> 0 us
  between operations: 21.1 us -> 0.01 us
  local copies, waits for them, and re-layouts: 21.7 us -> 6.13 us
  matrix products: 13.6 us -> 0 us
  loops' own time: 1.94 us -> 0 us
    pallas_call x0 -> x1, Pallas kernels: none -> 34.8 us  [per_device(): pl.pallas_call(functools.partial(kernel, nd, ny, nx, cap, unroll), out_sh...]
    ppermute x12 -> x0, waiting for transfers between devices: 28.2 us -> none  [the longest x6 19.2 us: extended(): lax.ppermute(tail, axis, [(i, (i + 1) % count) for i in range(count)])]
    ppermute x12 -> x0, starting transfers between devices: 16.8 us -> none  [the longest x6 10.1 us: extended(): lax.ppermute(head, axis, [((i + 1) % count, i) for i in range(count)])]
    dot_general x2 -> x0, matrix products: 13.6 us -> none  [the longest x1 8.36 us: per_device(): jnp.einsum('ptq,pq->pt', weight_blocks.astype(jnp.float32), picked, preci...]
    all_gather x3 -> x0, blocking collectives: 12.9 us -> none  [pad_tile(): gathered = lax.all_gather(top_row[None, :], 'gx', axis=1, tiled=True)[0]]
    another operation x5 -> x0, other arithmetic: 8.33 us -> none  [the longest x2 6.11 us: per_device(): heat_layers = jnp.stack(layer_sequence)]
    unnamed x1 -> x0, blocking collectives: 8.31 us -> none
    reduce_scatter x1 -> x0, waiting for transfers between devices: 7.25 us -> none  [per_device(): lax.psum_scatter(level_terms, 'depth', scatter_dimension=0, tiled=True)]
  transfers between devices with their start and end apart: 15 -> 0, of which waited for: 9 -> 0; matrix products, arithmetic and copies ran while one was open for 15% -> 0% of each run, Pallas kernels for 0% -> 0%
where the time goes in v1:
time: 41.2 us; the launch traced here: 40.9 us
  Pallas kernels  34.8 us (84%)
  local copies, waits for them, and re-layouts  6.13 us (15%)
    pallas_call x1, Pallas kernels, per_device(): pl.pallas_call(functools.partial(kernel, nd, ny, nx, cap, unroll), out_sh...  34.8 us
    unnamed x10, local copies, waits for them, and re-layouts  5.45 us

profile of v1, /device:TPU:0, one launch (start us, length us, event | category | flops | bytes accessed | tf_op | source)
XLA Modules:
  0.0 40.9 jit_solution(2737105536389865106)
XLA Ops:
  0.0 0.7 %copy.8 = s32[1,4,2,128]{3,1,2,0:T(4,128)S(1)} copy(s32[1,4,2,128]{3,2,1,0:T(2,128)} %bitcast.9) | data formatting | bytes 8192
  0.7 0.7 %reshape.10.tgt_v = s32[2,1,512]{2,1,0:T(1,128)S(1)} reshape(s32[1,1,2,512]{3,2,1,0:T(2,128)} %param.11) | data formatting | bytes 8192 | tf_op jit(solution)/shard_map/reshape | solution.py:477
  1.4 0.0 copy-start
  1.4 1.6 %copy-done = f32[4,512,256]{2,1,0:T(8,128)S(1)} copy-done((f32[4,512,256]{2,1,0:T(8,128)S(1)}, f32[4,512,256]{2,1,0:T(8,128)}, u32[]{:S(2)}) %copy-start) | copy-done | bytes 2097176
  3.0 0.0 copy-start.1
  3.0 1.0 %copy-done.1 = s32[512,256]{1,0:T(8,128)S(1)} copy-done((s32[512,256]{1,0:T(8,128)S(1)}, s32[512,256]{1,0:T(8,128)}, u32[]{:S(2)}) %copy-start.1) | copy-done | bytes 524312
  4.0 0.0 copy-start.2
  4.0 0.8 %copy-done.2 = f32[1,128,128]{2,1,0:T(8,128)S(1)} copy-done((f32[1,128,128]{2,1,0:T(8,128)S(1)}, f32[1,128,128]{2,1,0:T(8,128)}, u32[]{:S(2)}) %copy-start.2) | copy-done | bytes 65560
  4.9 0.0 copy-start.3
  4.9 0.7 %copy-done.3 = f32[4]{0:T(128)S(1)} copy-done((f32[4]{0:T(128)S(1)}, f32[4]{0:T(128)}, u32[]{:S(2)}) %copy-start.3) | copy-done | bytes 40
  5.5 34.8 %shard_map.73 = f32[128,128]{1,0:T(8,128)S(1)} custom-call(f32[4]{0:T(128)S(1)} %copy-done.3, s32[1024]{0:T(1024)S(1)} %bitcast.7, f32[4,512,256]{2,1,0:T(8,128)S(1)} %copy-done, s32[512,256]{1,0:T(8,128)S(1)} %copy-done.1, s32[2,1,512]{2,1,0:T(1,128)S(1)} %reshape.10.tgt_v, bf16[2,8192,128]{2,1,0:T(8,128)(2,1)} %bitcast.8, f32[128,128]{1,0:T(8,128)S(1)} %bitcast.6), custom_call_target="tpu_custom_call" | custom-call | tf_op jit(solution)/shard_map/pallas_call | solution.py:463
  40.3 0.6 %copy.10 = f32[1,128,128]{2,1,0:T(8,128)} copy(f32[1,128,128]{2,1,0:T(8,128)S(1)} %bitcast.5) | data formatting | bytes 131072
Async XLA Ops:
  1.4 1.6 %copy-start = (f32[4,512,256]{2,1,0:T(8,128)S(1)}, f32[4,512,256]{2,1,0:T(8,128)}, u32[]{:S(2)}) copy-start(f32[4,512,256]{2,1,0:T(8,128)} %temp_h.1) | copy-start | bytes 6291460
  3.0 1.0 %copy-start.1 = (s32[512,256]{1,0:T(8,128)S(1)}, s32[512,256]{1,0:T(8,128)}, u32[]{:S(2)}) copy-start(s32[512,256]{1,0:T(8,128)} %tally_v.1) | copy-start | bytes 1572868
  4.0 0.8 %copy-start.2 = (f32[1,128,128]{2,1,0:T(8,128)S(1)}, f32[1,128,128]{2,1,0:T(8,128)}, u32[]{:S(2)}) copy-start(f32[1,128,128]{2,1,0:T(8,128)} %param.13) | copy-start | bytes 196612
  4.9 0.7 %copy-start.3 = (f32[4]{0:T(128)S(1)}, f32[4]{0:T(128)}, u32[]{:S(2)}) copy-start(f32[4]{0:T(128)} %span_s.1) | copy-start | bytes 52

commit v2 on v1

--- a/solution.py
+++ b/solution.py
@@ -41,12 +41,13 @@
 
 def kernel(
     nd, ny, nx, cap, unroll,
-    span_s, pick_s, temp_h, tally_v, tgt_v, coef_h, base_v,
+    span_s, pick_h, temp_h, tally_h, tgt_h, coef_h, base_h,
     out_v,
+    pick_s, tally_v, tgt_v, tgt_rows, base_v,
     temp_v, coef_v, fa, fb, acoef, store, pack, pin, pint,
     col_out, col_in, row_out, row_in, th_out, th_in, prm,
     vout, vin, tslot, onehot, eexp,
-    temp_sem, coef_sem, col_ss, col_rs, row_ss, row_rs, th_ss, th_rs, tg_ss, tg_rs, v_ss, v_rs,
+    in_sem, temp_sem, coef_sem, col_ss, col_rs, row_ss, row_rs, th_ss, th_rs, tg_ss, tg_rs, v_ss, v_rs,
 ):
     d, y, b = lax.axis_index("depth"), lax.axis_index("gy"), lax.axis_index("gx")
     nl, rows, cols = temp_v.shape
@@ -56,6 +57,13 @@
     east, west = lax.rem(b + 1, nx), lax.rem(b + nx - 1, nx)
     mirror = nx - 1 - b
 
+    small = []
+    for n, (src, dst) in enumerate(
+        ((tally_h, tally_v), (tgt_h, tgt_v), (pick_h, pick_s), (base_h, base_v))
+    ):
+        copy = pltpu.make_async_copy(src, dst, in_sem.at[n])
+        copy.start()
+        small.append(copy)
     temp_copies = []
     for q in range(chunks):
         span = pl.ds(q * crow, crow)
@@ -91,14 +99,68 @@
     for l in range(1, nl):
         total = total + thick[l]
     th_out[...] = jnp.full(th_out.shape, total, F32)
-    zero_rows = jnp.zeros((PAD, cols), F32)
+    zero_rows = jnp.zeros((PAD, 128), F32)
     for m in range(5):
-        for buf in (fa, fb):
-            buf[m, 0:PAD, :] = zero_rows
-            buf[m, PAD + rows:, :] = zero_rows
+        for h in range(2):
+            for buf in (fa, fb):
+                buf[m, h, 0:PAD, :] = zero_rows
+                buf[m, h, PAD + rows:, :] = zero_rows
     pint[...] = jnp.zeros(pint.shape, F32)
     col_out[...] = jnp.zeros(col_out.shape, F32)
     row_out[...] = jnp.zeros(row_out.shape, F32)
+
+    lane = lanes((8, 128))
+    tall, high = 32, 64
+
+    def masks(count):
+        wide = lanes((count, 128))
+        return wide, wide == 0, wide == 127
+
+    def wet_rows(r, carry):
+        base = pl.multiple_of(r * high, high)
+        for h in range(2):
+            tally = tally_v[pl.ds(base, high), 128 * h:128 * h + 128]
+            fa[4, h, pl.ds(base + PAD, high), :] = jnp.where(tally > 0, 1.0, 0.0)
+        return carry
+
+    def neighbours(buf, m, base):
+        wide, first, final = masks(tall)
+        here = [buf[m, h, pl.ds(base + PAD, tall), :] for h in range(2)]
+        ahead = [pltpu.roll(x, 1, 1) for x in here]
+        behind = [pltpu.roll(x, 127, 1) for x in here]
+        left = [jnp.where(first, 0.0, ahead[0]), jnp.where(first, ahead[0], ahead[1])]
+        right = [jnp.where(final, behind[1], behind[0]), jnp.where(final, 0.0, behind[1])]
+        around = []
+        for h in range(2):
+            up = buf[m, h, pl.ds(base + PAD + 1, tall), :]
+            down = buf[m, h, pl.ds(base + PAD - 1, tall), :]
+            around.append((up + down) + (left[h] + right[h]))
+        return here, around
+
+    def count_rows(r, carry):
+        base = pl.multiple_of(r * tall, tall)
+        wet, count = neighbours(fa, 4, base)
+        for h in range(2):
+            acoef[h, pl.ds(base, tall), :] = 1.0 - smooth_nu * count[h]
+        return carry
+
+    tr = out_v.shape[0]
+
+    def build_onehot(j):
+        ids = tslot[j]
+        for q in range(8):
+            wanted = sublanes((tr, cap)) * 8 + q
+            onehot[q * tr:(q + 1) * tr, j * cap:(j + 1) * cap] = jnp.where(
+                wanted == ids, 1.0, 0.0
+            ).astype(BF16)
+
+    small[0].wait()
+    lax.fori_loop(0, rows // high, wet_rows, 0)
+    lax.fori_loop(0, rows // tall, count_rows, 0)
+    small[1].wait()
+    for j in range(nx):
+        tgt_rows[j] = tgt_v[j:j + 1, :]
+    tslot[0] = tgt_rows[b]
 
     inner = jnp.logical_and(y > 0, y < last)
 
@@ -121,11 +183,11 @@
     for j in range(1, nx):
         c = lax.rem(b + j, nx)
         copy = pltpu.make_async_remote_copy(
-            tgt_v.at[c], tslot.at[j], tg_ss.at[j], tg_rs.at[j], (d, y, c), MESH
+            tgt_rows.at[c], tslot.at[j], tg_ss.at[j], tg_rs.at[j], (d, y, c), MESH
         )
         copy.start()
         tg_copies.append(copy)
-    tslot[0] = tgt_v[b]
+    build_onehot(0)
 
     top = jnp.zeros((8, 128), F32)
     for i in range(1, nd):
@@ -142,54 +204,56 @@
         prm[l, 6] = jnp.full((8, 128), thick[l] / full_norm, F32)
         top = top + thick[l]
 
-    lane = lanes((8, 128))
-    first_lane, last_lane = lane == 0, lane == 127
-    row_tile = lambda r: pl.multiple_of(r * 8, 8)
-
-    def pack_edges(pairs):
-        packed = jnp.zeros((8, 128), F32)
-        for m, (left, right) in enumerate(pairs):
-            edge = jnp.where(first_lane, left, right)
-            packed = jnp.where((lane >> 1) == m, pltpu.roll(edge, 2 * m + 1, 1), packed)
+    def pack_edges(edges):
+        wide = lanes(edges[0].shape)
+        packed = jnp.zeros(edges[0].shape, F32)
+        for m, edge in enumerate(edges):
+            packed = jnp.where((wide >> 1) == m, pltpu.roll(edge, 2 * m + 1, 1), packed)
         return packed
 
     def heat_rows(r, carry):
-        base = row_tile(r)
-        pairs = [[None, None] for _ in range(5)]
+        base = pl.multiple_of(r * tall, tall)
+        first = masks(tall)[1]
+        fields = []
         for h in range(2):
-            here = (pl.ds(base, 8), slice(128 * h, 128 * h + 128))
+            here = (pl.ds(base, tall), slice(128 * h, 128 * h + 128))
             tally = tally_v[here]
             sums = [None] * 4
             for l in range(nl):
+                par = [jnp.concatenate([prm[l, n]] * (tall // 8), axis=0) for n in range(7)]
                 t = temp_v[(l,) + here]
                 expand = 1.0 + t * (therm_one + therm_two * t)
-                heat = (t + prm[l, 0] * expand - prm[l, 1]) / (expand - prm[l, 2])
+                heat = (t + par[0] * expand - par[1]) / (expand - par[2])
                 heat = jnp.where(d * nl + l < tally, heat, 0.0)
                 for k in range(4):
-                    term = prm[l, 3 + k] * heat
+                    term = par[3 + k] * heat
                     sums[k] = term if l == 0 else sums[k] + term
-            sums.append(jnp.where(tally > 0, 1.0, 0.0))
-            for m in range(5):
-                fa[m, pl.ds(base + PAD, 8), 128 * h:128 * h + 128] = sums[m]
-                pairs[m][h] = sums[m]
-        pack[pl.ds(base, 8), :] = pack_edges(pairs)
+            for k in range(4):
+                fa[k, h, pl.ds(base + PAD, tall), :] = sums[k]
+            sums.append(fa[4, h, pl.ds(base + PAD, tall), :])
+            fields.append(sums)
+        pack[pl.ds(base, tall), :] = pack_edges(
+            [jnp.where(first, fields[0][m], fields[1][m]) for m in range(5)]
+        )
         return carry
 
     for q in range(chunks):
         temp_copies[q].wait()
-        lax.fori_loop(q * crow // 8, (q + 1) * crow // 8, heat_rows, 0, unroll=2)
+        lax.fori_loop(q * crow // tall, (q + 1) * crow // tall, heat_rows, 0)
 
     def send_edges(e, buf):
         for q in range(rows // 128):
             span = slice(128 * q, 128 * q + 128)
-            turned = pack[span, :].T
+            turned = pack[span, 0:16].T
             for m in range(5):
                 col_out[e, 0, m:m + 1, span] = turned[2 * m:2 * m + 1]
                 col_out[e, 1, m:m + 1, span] = turned[2 * m + 1:2 * m + 2]
         for m in range(5):
             src = fa if m == 4 else buf
-            row_out[e, 0, m:m + 1, :] = src[m, PAD + rows - 1:PAD + rows, :]
-            row_out[e, 1, m:m + 1, :] = src[m, PAD:PAD + 1, :]
+            for h in range(2):
+                half = slice(128 * h, 128 * h + 128)
+                row_out[e, 0, m:m + 1, half] = src[m, h, PAD + rows - 1:PAD + rows, :]
+                row_out[e, 1, m:m + 1, half] = src[m, h, PAD:PAD + 1, :]
         to_east = pltpu.make_async_remote_copy(
             col_out.at[e, 0], col_in.at[e, 0], col_ss.at[e, 0], col_rs.at[e, 0], (d, y, east), MESH
         )
@@ -249,97 +313,89 @@
             pint[2 * m + 1:2 * m + 2, :] = col_in[e, 0, m:m + 1, :]
         for q in range(rows // 128):
             span = slice(128 * q, 128 * q + 128)
-            pin[span, :] = pint[:, span].T
-
-    tall = 32
-
-    def neighbours(buf, m, base):
-        wide = lanes((tall, cols))
-        around = buf[m, pl.ds(base, tall + 2 * PAD), :]
-        here = around[PAD:PAD + tall]
-        up = around[PAD + 1:PAD + 1 + tall]
-        down = around[PAD - 1:PAD - 1 + tall]
-        left = jnp.where(wide == 0, 0.0, pltpu.roll(here, 1, 1))
-        right = jnp.where(wide == cols - 1, 0.0, pltpu.roll(here, cols - 1, 1))
-        return here, (up + down) + (left + right)
-
-    def sweep(src, dst, build):
+            pin[span, 0:16] = pint[:, span].T
+
+    def sweep(src, dst):
         def body(r, carry):
             base = pl.multiple_of(r * tall, tall)
-            if build:
-                wet, count = neighbours(fa, 4, base)
-                keep = 1.0 - smooth_nu * count
-                acoef[pl.ds(base, tall), :] = keep
-            else:
-                wet = fa[4, pl.ds(base + PAD, tall), :]
-                keep = acoef[pl.ds(base, tall), :]
-            gain = smooth_nu * wet
+            keep = [acoef[h, pl.ds(base, tall), :] for h in range(2)]
+            gain = [smooth_nu * fa[4, h, pl.ds(base + PAD, tall), :] for h in range(2)]
             for k in range(4):
                 here, around = neighbours(src, k, base)
-                dst[k, pl.ds(base + PAD, tall), :] = keep * here + gain * around
+                for h in range(2):
+                    dst[k, h, pl.ds(base + PAD, tall), :] = keep[h] * here[h] + gain[h] * around[h]
             return carry
 
         lax.fori_loop(0, rows // tall, body, 0)
 
     def fix_rows(e, src, dst):
         for side, row in ((0, PAD + rows - 1), (1, PAD)):
-            wet_edge = row_in[e, side, 4:5, :]
-            gain = smooth_nu * fa[4, row:row + 1, :]
-            for k in range(4):
-                more = gain * (row_in[e, side, k:k + 1, :] - wet_edge * src[k, row:row + 1, :])
-                dst[k, row:row + 1, :] = dst[k, row:row + 1, :] + more
+            for h in range(2):
+                half = slice(128 * h, 128 * h + 128)
+                wet_edge = row_in[e, side, 4:5, half]
+                gain = smooth_nu * fa[4, h, row:row + 1, :]
+                for k in range(4):
+                    more = gain * (row_in[e, side, k:k + 1, half] - wet_edge * src[k, h, row:row + 1, :])
+                    dst[k, h, row:row + 1, :] = dst[k, h, row:row + 1, :] + more
 
     def fix_columns(src, dst, base):
-        here = pl.ds(base + PAD, 8)
-        edges = pin[pl.ds(base, 8), :]
+        wide, first, final = masks(high)
+        here = pl.ds(base + PAD, high)
+        edges = pin[pl.ds(base, high), :]
         wet_edge = pltpu.roll(edges, 128 - 9, 1)
+        wet = jnp.where(first, fa[4, 0, here, :], fa[4, 1, here, :])
+        gain = jnp.where(jnp.logical_or(first, final), smooth_nu * wet, 0.0)
         fixed = []
         for k in range(4):
             field_edge = pltpu.roll(edges, 128 - (2 * k + 1), 1)
-            pair = []
-            for h, mask in ((0, first_lane), (1, last_lane)):
-                at = (k, here, slice(128 * h, 128 * h + 128))
-                gain = smooth_nu * fa[(4,) + at[1:]]
-                more = gain * (field_edge - wet_edge * src[at])
-                pair.append(dst[at] + jnp.where(mask, more, 0.0))
-            fixed.append(pair)
-        return fixed
+            old = jnp.where(first, src[k, 0, here, :], src[k, 1, here, :])
+            more = gain * (field_edge - wet_edge * old)
+            fixed.append(
+                [
+                    dst[k, 0, here, :] + jnp.where(first, more, 0.0),
+                    dst[k, 1, here, :] + jnp.where(final, more, 0.0),
+                ]
+            )
+        return fixed, wet
 
     edges = send_edges(0, fa)
-    sweep(fa, fb, True)
+    sweep(fa, fb)
     receive_edges(0, edges)
     fix_rows(0, fa, fb)
 
     def fix_first(r, carry):
-        base = row_tile(r)
-        fixed = fix_columns(fa, fb, base)
+        base = pl.multiple_of(r * high, high)
+        first = masks(high)[1]
+        fixed, wet = fix_columns(fa, fb, base)
         for k in range(4):
             for h in range(2):
-                fb[k, pl.ds(base + PAD, 8), 128 * h:128 * h + 128] = fixed[k][h]
-        wet = [fa[4, pl.ds(base + PAD, 8), 128 * h:128 * h + 128] for h in range(2)]
-        pack[pl.ds(base, 8), :] = pack_edges(fixed + [wet])
+                fb[k, h, pl.ds(base + PAD, high), :] = fixed[k][h]
+        pack[pl.ds(base, high), :] = pack_edges(
+            [jnp.where(first, fixed[k][0], fixed[k][1]) for k in range(4)] + [wet]
+        )
         return carry
 
-    lax.fori_loop(0, rows // 8, fix_first, 0, unroll=2)
+    lax.fori_loop(0, rows // high, fix_first, 0)
     edges = send_edges(1, fb)
-    sweep(fb, fa, False)
+    sweep(fb, fa)
     receive_edges(1, edges)
     fix_rows(1, fb, fa)
 
     def fix_second(r, carry):
-        base = row_tile(r)
-        fixed = fix_columns(fb, fa, base)
+        base = pl.multiple_of(r * high, high)
+        fixed, _ = fix_columns(fb, fa, base)
         for h in range(2):
-            parts = []
-            for k in range(4):
-                parts.append(fixed[k][h].astype(BF16).astype(F32))
-            for k in range(4):
-                parts.append(fixed[k][h] - parts[k])
-            block = jnp.swapaxes(jnp.stack(parts), 0, 1)
-            store[pl.ds(h * rows + base, 8)] = block
+            parts = [fixed[k][h].astype(BF16).astype(F32) for k in range(4)]
+            parts += [fixed[k][h] - parts[k] for k in range(4)]
+            for n in range(0, high, 8):
+                block = jnp.swapaxes(jnp.stack([part[n:n + 8] for part in parts]), 0, 1)
+                for m in range(8):
+                    store[2 * (base + n + m) + h] = block[m]
         return carry
 
-    lax.fori_loop(0, rows // 8, fix_second, 0, unroll=2)
+    lax.fori_loop(0, rows // high, fix_second, 0)
+    for copy in small[2:]:
+        copy.wait()
 
     group = lane >> 4
     v_copies = []
@@ -352,8 +408,7 @@
                 g = u * unroll + s
                 picked = []
                 for p in range(16):
-                    at = pick_s[c * cap + g * 16 + p]
-                    picked.append(store[(at & 1) * rows + (at >> 1)])
+                    picked.append(store[pick_s[c, g * 16 + p]])
                 block = jnp.concatenate(picked, axis=0).astype(BF16)
                 weights = coef_v[j, pl.ds(pl.multiple_of(g * 256, 256), 256), :]
                 prod = lax.dot_general(
@@ -383,15 +438,8 @@
 
     for copy in tg_copies:
         copy.wait()
-    tr = out_v.shape[0]
-    for j in range(nx):
-        ids = tslot[j]
-        for q in range(8):
-            shape = (tr, cap)
-            wanted = sublanes(shape) * 8 + q
-            onehot[q * tr:(q + 1) * tr, j * cap:(j + 1) * cap] = jnp.where(
-                wanted == ids, 1.0, 0.0
-            ).astype(BF16)
+    for j in range(1, nx):
+        build_onehot(j)
     for copy in v_copies:
         copy.wait()
     gr = cap // 8
@@ -431,15 +479,20 @@
     sspec = pl.BlockSpec(memory_space=pltpu.SMEM)
     tr, tc = base.shape[1:]
     scratch = [
+        pltpu.SMEM((nx, cap), jnp.int32),
+        vmem((rows, cols), jnp.int32),
+        vmem((nx, cap), jnp.int32),
+        vmem((nx, 1, cap), jnp.int32),
+        vmem((tr, tc), F32),
         vmem((nl, rows, cols), F32),
         vmem((nx, cap * TB, SB), BF16),
-        vmem((5, rows + 2 * PAD, cols), F32),
-        vmem((5, rows + 2 * PAD, cols), F32),
-        vmem((rows, cols), F32),
+        vmem((5, 2, rows + 2 * PAD, 128), F32),
+        vmem((5, 2, rows + 2 * PAD, 128), F32),
+        vmem((2, rows, 128), F32),
         vmem((blocks, 8, SB), F32),
         vmem((rows, 128), F32),
         vmem((rows, 128), F32),
-        vmem((128, rows), F32),
+        vmem((16, rows), F32),
         vmem((2, 2, 8, rows), F32),
         vmem((2, 2, 8, rows), F32),
         vmem((2, 2, 8, cols), F32),
@@ -453,6 +506,7 @@
         vmem((8 * tr, nx * cap), BF16),
         vmem((nx * cap, 256), BF16),
         dma((4,)),
+        dma((4,)),
         dma((nx,)),
         dma((2, 2)), dma((2, 2)),
         dma((2, 2)), dma((2, 2)),
@@ -463,18 +517,18 @@
     out = pl.pallas_call(
         functools.partial(kernel, nd, ny, nx, cap, unroll),
         out_shape=jax.ShapeDtypeStruct((tr, tc), F32),
-        in_specs=[sspec, sspec, any_spec, vspec, vspec, any_spec, vspec],
+        in_specs=[sspec] + [any_spec] * 6,
         out_specs=vspec,
         scratch_shapes=scratch,
         compiler_params=pltpu.CompilerParams(
-            collective_id=0, has_side_effects=True, vmem_limit_bytes=48 * 1024 * 1024
+            collective_id=0, has_side_effects=True, vmem_limit_bytes=60 * 1024 * 1024
         ),
     )(
         span,
-        sender.reshape(-1),
+        sender.reshape(nx, cap),
         temp,
         tally,
-        receiver.reshape(nx, 1, cap),
+        receiver.reshape(nx, cap),
         coef.reshape(nx, cap * TB, SB),
         base[0],
     )

time: 41.2 us -> 31.2 us (0.76)
  Pallas kernels: 34.8 us -> 29.6 us
  local copies, waits for them, and re-layouts: 6.13 us -> 1.47 us
    pallas_call x1, Pallas kernels: 34.8 us -> 29.6 us  [per_device(): pl.pallas_call(functools.partial(kernel, nd, ny, nx, cap, unroll), out_sh...]
    unnamed x10 -> x1, local copies, waits for them, and re-layouts: 5.45 us -> 1.47 us
    reshape x1 -> x0, local copies, waits for them, and re-layouts: 0.69 us -> none  [per_device(): receiver.reshape(nx, 1, cap)]
where the time goes in v2:
time: 31.2 us; the launch traced here: 31 us
  Pallas kernels  29.6 us (95%)
  local copies, waits for them, and re-layouts  1.47 us (5%)
    pallas_call x1, Pallas kernels, per_device(): pl.pallas_call(functools.partial(kernel, nd, ny, nx, cap, unroll), out_sh...  29.6 us
    unnamed x1, local copies, waits for them, and re-layouts  1.47 us

profile of v2, /device:TPU:0, one launch (start us, length us, event | category | flops | bytes accessed | tf_op | source)
XLA Modules:
  0.0 31.0 jit_solution(5976934413541787389)
XLA Ops:
  0.0 29.6 %shard_map.73 = f32[128,128]{1,0:T(8,128)} custom-call(f32[4]{0:T(128)} %span_s.1, s32[2,512]{1,0:T(2,128)} %bitcast.8, f32[4,512,256]{2,1,0:T(8,128)} %temp_h.1, s32[512,256]{1,0:T(8,128)} %tally_h.1, s32[2,512]{1,0:T(2,128)} %bitcast.9, bf16[2,8192,128]{2,1,0:T(8,128)(2,1)} %bitcast.5, f32[128,128]{1,0:T(8,128)} %bitcast.7), custom_call_target="tpu_custom_call" | custom-call | tf_op jit(solution)/shard_map/pallas_call | solution.py:517
  29.6 1.5 %copy.9 = f32[1,128,128]{2,1,0:T(8,128)} copy(f32[1,128,128]{2,1,0:T(8,128)} %bitcast.6) | data formatting | bytes 131072

commit v3 on v2

--- a/solution.py
+++ b/solution.py
@@ -23,6 +23,7 @@
 F32 = jnp.float32
 BF16 = jnp.bfloat16
 PAD = 8
+PITCH = 9
 
 
 def lanes(shape):
@@ -43,7 +44,7 @@
     nd, ny, nx, cap, unroll,
     span_s, pick_h, temp_h, tally_h, tgt_h, coef_h, base_h,
     out_v,
-    pick_s, tally_v, tgt_v, tgt_rows, base_v,
+    pick_v, pick_s, tally_v, tgt_v, tgt_rows, base_v,
     temp_v, coef_v, fa, fb, acoef, store, pack, pin, pint,
     col_out, col_in, row_out, row_in, th_out, th_in, prm,
     vout, vin, tslot, onehot, eexp,
@@ -59,7 +60,7 @@
 
     small = []
     for n, (src, dst) in enumerate(
-        ((tally_h, tally_v), (tgt_h, tgt_v), (pick_h, pick_s), (base_h, base_v))
+        ((tally_h, tally_v), (tgt_h, tgt_v), (pick_h, pick_v), (base_h, base_v))
     ):
         copy = pltpu.make_async_copy(src, dst, in_sem.at[n])
         copy.start()
@@ -110,7 +111,7 @@
     row_out[...] = jnp.zeros(row_out.shape, F32)
 
     lane = lanes((8, 128))
-    tall, high = 32, 64
+    tall, high = 64, 128
 
     def masks(count):
         wide = lanes((count, 128))
@@ -156,7 +157,10 @@
 
     small[0].wait()
     lax.fori_loop(0, rows // high, wet_rows, 0)
-    lax.fori_loop(0, rows // tall, count_rows, 0)
+    small[2].wait()
+    pick_v[...] = (pick_v[...] & 1) * (rows * PITCH) + (pick_v[...] >> 1) * PITCH
+    offsets = pltpu.make_async_copy(pick_v, pick_s, in_sem.at[4])
+    offsets.start()
     small[1].wait()
     for j in range(nx):
         tgt_rows[j] = tgt_v[j:j + 1, :]
@@ -187,6 +191,7 @@
         )
         copy.start()
         tg_copies.append(copy)
+    lax.fori_loop(0, rows // tall, count_rows, 0)
     build_onehot(0)
 
     top = jnp.zeros((8, 128), F32)
@@ -388,14 +393,14 @@
             parts = [fixed[k][h].astype(BF16).astype(F32) for k in range(4)]
             parts += [fixed[k][h] - parts[k] for k in range(4)]
             for n in range(0, high, 8):
-                block = jnp.swapaxes(jnp.stack([part[n:n + 8] for part in parts]), 0, 1)
+                start = (h * rows + n) * PITCH + base * PITCH
                 for m in range(8):
-                    store[2 * (base + n + m) + h] = block[m]
+                    store[pl.ds(start + m, 8, stride=PITCH), :] = parts[m][n:n + 8]
         return carry
 
     lax.fori_loop(0, rows // high, fix_second, 0)
-    for copy in small[2:]:
-        copy.wait()
+    small[3].wait()
+    offsets.wait()
 
     group = lane >> 4
     v_copies = []
@@ -408,7 +413,7 @@
                 g = u * unroll + s
                 picked = []
                 for p in range(16):
-                    picked.append(store[pick_s[c, g * 16 + p]])
+                    picked.append(store[pl.ds(pick_s[c, g * 16 + p], 8), :])
                 block = jnp.concatenate(picked, axis=0).astype(BF16)
                 weights = coef_v[j, pl.ds(pl.multiple_of(g * 256, 256), 256), :]
                 prod = lax.dot_general(
@@ -427,6 +432,7 @@
             return carry
 
         lax.fori_loop(0, cap // (16 * unroll), remap, 0)
+        copies = []
         for i in range(nd):
             if (i, j) != (0, 0):
                 copy = pltpu.make_async_remote_copy(
@@ -434,17 +440,19 @@
                     (lax.rem(d + i, nd), y, c), MESH,
                 )
                 copy.start()
-                v_copies.append(copy)
+                copies.append(copy)
+        v_copies.append((j, copies))
 
     for copy in tg_copies:
         copy.wait()
     for j in range(1, nx):
         build_onehot(j)
-    for copy in v_copies:
-        copy.wait()
     gr = cap // 8
     own_group = (lanes((gr, 8, 128)) >> 4) == lax.broadcasted_iota(jnp.int32, (gr, 8, 128), 1)
-    for j in range(nx):
+    both = None
+    for j, copies in v_copies:
+        for copy in copies:
+            copy.wait()
         summed = vout[0, 0] if j == 0 else vin[0, j]
         for i in range(1, nd):
             summed = summed + vin[i, j]
@@ -452,7 +460,9 @@
         hi, lo = split_two(spread)
         eexp[j * cap:(j + 1) * cap, 0:128] = hi
         eexp[j * cap:(j + 1) * cap, 128:256] = lo
-    both = jnp.dot(onehot[...], eexp[...], preferred_element_type=F32)
+        span = slice(j * cap, (j + 1) * cap)
+        part = jnp.dot(onehot[:, span], eexp[span, :], preferred_element_type=F32)
+        both = part if both is None else both + part
     hi, lo = split_two(both[:, 0:128] + both[:, 128:256])
     shape = (128, 128)
     tile16 = jnp.where((lanes(shape) & 15) == (sublanes(shape) & 15), 1.0, 0.0).astype(BF16)
@@ -470,7 +480,7 @@
     nd, ny, nx = sizes
     nl, rows, cols = temp.shape
     cap = sender.shape[-1]
-    unroll = min(8, cap // 16)
+    unroll = min(16, cap // 16)
     blocks = rows * cols // SB
     vmem = pltpu.VMEM
     dma = pltpu.SemaphoreType.DMA
@@ -479,6 +489,7 @@
     sspec = pl.BlockSpec(memory_space=pltpu.SMEM)
     tr, tc = base.shape[1:]
     scratch = [
+        vmem((nx, cap), jnp.int32),
         pltpu.SMEM((nx, cap), jnp.int32),
         vmem((rows, cols), jnp.int32),
         vmem((nx, cap), jnp.int32),
@@ -489,7 +500,7 @@
         vmem((5, 2, rows + 2 * PAD, 128), F32),
         vmem((5, 2, rows + 2 * PAD, 128), F32),
         vmem((2, rows, 128), F32),
-        vmem((blocks, 8, SB), F32),
+        vmem((blocks * PITCH, SB), F32),
         vmem((rows, 128), F32),
         vmem((rows, 128), F32),
         vmem((16, rows), F32),
@@ -505,7 +516,7 @@
         vmem((nx, 1, cap), jnp.int32),
         vmem((8 * tr, nx * cap), BF16),
         vmem((nx * cap, 256), BF16),
-        dma((4,)),
+        dma((5,)),
         dma((4,)),
         dma((nx,)),
         dma((2, 2)), dma((2, 2)),

time: 31.2 us -> 28.3 us (0.907)
  Pallas kernels: 29.6 us -> 26.6 us
    pallas_call x1, Pallas kernels: 29.6 us -> 26.6 us  [per_device(): pl.pallas_call(functools.partial(kernel, nd, ny, nx, cap, unroll), out_sh...]
where the time goes in v3:
time: 28.3 us; the launch traced here: 28.1 us
  Pallas kernels  26.6 us (94%)
  local copies, waits for them, and re-layouts  1.47 us (5%)
    pallas_call x1, Pallas kernels, per_device(): pl.pallas_call(functools.partial(kernel, nd, ny, nx, cap, unroll), out_sh...  26.6 us
    unnamed x1, local copies, waits for them, and re-layouts  1.47 us

profile of v3, /device:TPU:0, one launch (start us, length us, event | category | flops | bytes accessed | tf_op | source)
XLA Modules:
  0.0 28.1 jit_solution(2200563616173686903)
XLA Ops:
  0.0 26.6 %shard_map.73 = f32[128,128]{1,0:T(8,128)} custom-call(f32[4]{0:T(128)} %span_s.1, s32[2,512]{1,0:T(2,128)} %bitcast.8, f32[4,512,256]{2,1,0:T(8,128)} %temp_h.1, s32[512,256]{1,0:T(8,128)} %tally_h.1, s32[2,512]{1,0:T(2,128)} %bitcast.9, bf16[2,8192,128]{2,1,0:T(8,128)(2,1)} %bitcast.5, f32[128,128]{1,0:T(8,128)} %bitcast.7), custom_call_target="tpu_custom_call" | custom-call | tf_op jit(solution)/shard_map/pallas_call | solution.py:528
  26.6 1.5 %copy.9 = f32[1,128,128]{2,1,0:T(8,128)} copy(f32[1,128,128]{2,1,0:T(8,128)} %bitcast.6) | data formatting | bytes 131072

commit v4 on v3

--- a/solution.py
+++ b/solution.py
@@ -41,10 +41,10 @@
 
 
 def kernel(
-    nd, ny, nx, cap, unroll,
-    span_s, pick_h, temp_h, tally_h, tgt_h, coef_h, base_h,
+    nd, ny, nx, cap, unroll, parts,
+    span_h, pick_h, temp_h, tally_h, tgt_h, coef_h, base_h,
     out_v,
-    pick_v, pick_s, tally_v, tgt_v, tgt_rows, base_v,
+    span_s, pick_v, pick_s, tally_v, tgt_v, tgt_rows, base_v,
     temp_v, coef_v, fa, fb, acoef, store, pack, pin, pint,
     col_out, col_in, row_out, row_in, th_out, th_in, prm,
     vout, vin, tslot, onehot, eexp,
@@ -60,7 +60,7 @@
 
     small = []
     for n, (src, dst) in enumerate(
-        ((tally_h, tally_v), (tgt_h, tgt_v), (pick_h, pick_v), (base_h, base_v))
+        ((tally_h, tally_v), (tgt_h, tgt_v), (pick_h, pick_v), (base_h, base_v), (span_h, span_s))
     ):
         copy = pltpu.make_async_copy(src, dst, in_sem.at[n])
         copy.start()
@@ -95,6 +95,7 @@
     def _():
         pl.semaphore_signal(barrier, inc=1, device_id=(d, y + 1, b), device_id_type=MESH)
 
+    small[4].wait()
     thick = [span_s[l] for l in range(nl)]
     total = thick[0]
     for l in range(1, nl):
@@ -159,7 +160,7 @@
     lax.fori_loop(0, rows // high, wet_rows, 0)
     small[2].wait()
     pick_v[...] = (pick_v[...] & 1) * (rows * PITCH) + (pick_v[...] >> 1) * PITCH
-    offsets = pltpu.make_async_copy(pick_v, pick_s, in_sem.at[4])
+    offsets = pltpu.make_async_copy(pick_v, pick_s, in_sem.at[5])
     offsets.start()
     small[1].wait()
     for j in range(nx):
@@ -203,7 +204,7 @@
         press = top + 0.5 * thick[l]
         prm[l, 0] = alpha * press
         prm[l, 1] = (0.5 * alpha * compress) * press * press
-        prm[l, 2] = compress * press
+        prm[l, 2] = 1.0 - compress * press
         for k, depth in enumerate(bounds):
             prm[l, 3 + k] = jnp.clip(depth - top, 0.0, thick[l]) / depth
         prm[l, 6] = jnp.full((8, 128), thick[l] / full_norm, F32)
@@ -227,8 +228,7 @@
             for l in range(nl):
                 par = [jnp.concatenate([prm[l, n]] * (tall // 8), axis=0) for n in range(7)]
                 t = temp_v[(l,) + here]
-                expand = 1.0 + t * (therm_one + therm_two * t)
-                heat = (t + par[0] * expand - par[1]) / (expand - par[2])
+                heat = par[0] + (t + par[1]) / (par[2] + t * (therm_one + therm_two * t))
                 heat = jnp.where(d * nl + l < tally, heat, 0.0)
                 for k in range(4):
                     term = par[3 + k] * heat
@@ -411,36 +411,34 @@
         def remap(u, carry, c=c, j=j):
             for s in range(unroll):
                 g = u * unroll + s
-                picked = []
-                for p in range(16):
-                    picked.append(store[pl.ds(pick_s[c, g * 16 + p], 8), :])
+                picked = [store[pl.ds(pick_s[c, g * 8 + p], 8), :] for p in range(8)]
                 block = jnp.concatenate(picked, axis=0).astype(BF16)
-                weights = coef_v[j, pl.ds(pl.multiple_of(g * 256, 256), 256), :]
+                weights = coef_v[j, pl.ds(pl.multiple_of(g * 128, 128), 128), :]
                 prod = lax.dot_general(
                     block, weights, (((1,), (1,)), ((), ())), preferred_element_type=F32
                 )
-                for half in range(2):
-                    tight = jnp.zeros((8, 128), F32)
-                    for p in range(8):
-                        row = (half * 8 + p) * 8
-                        tight = jnp.where(
-                            group == p, prod[row:row + 8, 128 * half:128 * half + 128], tight
-                        )
-                    tight = tight[0:4] + tight[4:8]
-                    for k in range(4):
-                        vout[lax.rem(k - d + nd, nd), j, pl.ds(g * 2 + half, 1), :] = tight[k:k + 1]
+                tight = prod[0:8]
+                for p in range(1, 8):
+                    tight = jnp.where(group == p, prod[p * 8:p * 8 + 8], tight)
+                tight = tight[0:4] + tight[4:8]
+                for k in range(4):
+                    vout[lax.rem(k - d + nd, nd), j, pl.ds(g, 1), :] = tight[k:k + 1]
             return carry
 
-        lax.fori_loop(0, cap // (16 * unroll), remap, 0)
         copies = []
-        for i in range(nd):
-            if (i, j) != (0, 0):
-                copy = pltpu.make_async_remote_copy(
-                    vout.at[i, j], vin.at[i, j], v_ss.at[i, j], v_rs.at[i, j],
-                    (lax.rem(d + i, nd), y, c), MESH,
-                )
-                copy.start()
-                copies.append(copy)
+        steps = cap // (8 * unroll)
+        for part in range(parts):
+            lax.fori_loop(part * steps // parts, (part + 1) * steps // parts, remap, 0)
+            span = pl.ds(part * (cap // 8 // parts), cap // 8 // parts)
+            for i in range(nd):
+                if (i, j) != (0, 0):
+                    copy = pltpu.make_async_remote_copy(
+                        vout.at[i, j, span, :], vin.at[i, j, span, :],
+                        v_ss.at[i, j, part], v_rs.at[i, j, part],
+                        (lax.rem(d + i, nd), y, c), MESH,
+                    )
+                    copy.start()
+                    copies.append(copy)
         v_copies.append((j, copies))
 
     for copy in tg_copies:
@@ -480,15 +478,16 @@
     nd, ny, nx = sizes
     nl, rows, cols = temp.shape
     cap = sender.shape[-1]
-    unroll = min(16, cap // 16)
+    parts = 2 if cap % 256 == 0 else 1
+    unroll = min(32, cap // 8 // parts)
     blocks = rows * cols // SB
     vmem = pltpu.VMEM
     dma = pltpu.SemaphoreType.DMA
     any_spec = pl.BlockSpec(memory_space=pl.ANY)
     vspec = pl.BlockSpec(memory_space=vmem)
-    sspec = pl.BlockSpec(memory_space=pltpu.SMEM)
     tr, tc = base.shape[1:]
     scratch = [
+        pltpu.SMEM((span.shape[0],), F32),
         vmem((nx, cap), jnp.int32),
         pltpu.SMEM((nx, cap), jnp.int32),
         vmem((rows, cols), jnp.int32),
@@ -516,32 +515,37 @@
         vmem((nx, 1, cap), jnp.int32),
         vmem((8 * tr, nx * cap), BF16),
         vmem((nx * cap, 256), BF16),
-        dma((5,)),
+        dma((6,)),
         dma((4,)),
         dma((nx,)),
         dma((2, 2)), dma((2, 2)),
         dma((2, 2)), dma((2, 2)),
         dma((nd,)), dma((nd,)),
         dma((nx,)), dma((nx,)),
-        dma((nd, nx)), dma((nd, nx)),
+        dma((nd, nx, parts)), dma((nd, nx, parts)),
     ]
     out = pl.pallas_call(
-        functools.partial(kernel, nd, ny, nx, cap, unroll),
-        out_shape=jax.ShapeDtypeStruct((tr, tc), F32),
-        in_specs=[sspec] + [any_spec] * 6,
+        functools.partial(kernel, nd, ny, nx, cap, unroll, parts),
+        out_shape=pltpu.VMEM((tr, tc), F32),
+        in_specs=[any_spec] * 7,
         out_specs=vspec,
         scratch_shapes=scratch,
         compiler_params=pltpu.CompilerParams(
-            collective_id=0, has_side_effects=True, vmem_limit_bytes=60 * 1024 * 1024
+            collective_id=0, has_side_effects=True, vmem_limit_bytes=48 * 1024 * 1024
         ),
     )(
-        span,
-        sender.reshape(nx, cap),
-        temp,
-        tally,
-        receiver.reshape(nx, cap),
-        coef.reshape(nx, cap * TB, SB),
-        base[0],
+        *[
+            pltpu.with_memory_space_constraint(x, pltpu.HBM)
+            for x in (
+                span,
+                sender.reshape(nx, cap),
+                temp,
+                tally,
+                receiver.reshape(nx, cap),
+                coef.reshape(nx, cap * TB, SB),
+                base[0],
+            )
+        ],
     )
     return out[None]
 

time: 28.3 us -> 26.3 us (0.929)
  Pallas kernels: 26.6 us -> 25.5 us
  local copies, waits for them, and re-layouts: 1.47 us -> 0.63 us
    pallas_call x1, Pallas kernels: 26.6 us -> 25.5 us  [per_device(): pl.pallas_call(functools.partial(kernel, nd, ny, nx, cap, unroll, parts),...]
    unnamed x1, local copies, waits for them, and re-layouts: 1.47 us -> 0.63 us
where the time goes in v4:
time: 26.3 us; the launch traced here: 26.2 us
  Pallas kernels  25.5 us (97%)
  local copies, waits for them, and re-layouts  0.63 us (2%)
    pallas_call x1, Pallas kernels, per_device(): pl.pallas_call(functools.partial(kernel, nd, ny, nx, cap, unroll, parts),...  25.5 us
    unnamed x1, local copies, waits for them, and re-layouts  0.63 us

profile of v4, /device:TPU:0, one launch (start us, length us, event | category | flops | bytes accessed | tf_op | source)
XLA Modules:
  0.0 26.2 jit_solution(3961938197465507086)
XLA Ops:
  0.0 25.5 %shard_map.73 = f32[128,128]{1,0:T(8,128)S(1)} custom-call(f32[4]{0:T(128)} %span_h.1, s32[2,512]{1,0:T(2,128)} %bitcast.8, f32[4,512,256]{2,1,0:T(8,128)} %temp_h.1, s32[512,256]{1,0:T(8,128)} %tally_h.1, s32[2,512]{1,0:T(2,128)} %bitcast.9, bf16[2,8192,128]{2,1,0:T(8,128)(2,1)} %bitcast.6, f32[128,128]{1,0:T(8,128)} %bitcast.7), custom_call_target="tpu_custom_call" | custom-call | tf_op jit(solution)/shard_map/pallas_call | solution.py:527
  25.5 0.6 %copy.9 = f32[1,128,128]{2,1,0:T(8,128)} copy(f32[1,128,128]{2,1,0:T(8,128)S(1)} %bitcast.5) | data formatting | bytes 131072

commit v5 on v4

--- a/solution.py
+++ b/solution.py
@@ -167,6 +167,75 @@
         tgt_rows[j] = tgt_v[j:j + 1, :]
     tslot[0] = tgt_rows[b]
 
+    def pack_edges(edges):
+        wide = lanes(edges[0].shape)
+        packed = jnp.zeros(edges[0].shape, F32)
+        for m, edge in enumerate(edges):
+            packed = jnp.where((wide >> 1) == m, pltpu.roll(edge, 2 * m + 1, 1), packed)
+        return packed
+
+    def raw_rows(r, carry):
+        base = pl.multiple_of(r * high, high)
+        first = masks(high)[1]
+        here = pl.ds(base, high)
+        edges = [
+            jnp.where(first, temp_v[l, here, 0:128], temp_v[l, here, 128:256]) for l in range(nl)
+        ]
+        tally = jnp.where(first, tally_v[here, 0:128], tally_v[here, 128:256])
+        pack[here, :] = pack_edges(edges + [tally.astype(F32)])
+        return carry
+
+    for copy in temp_copies:
+        copy.wait()
+    lax.fori_loop(0, rows // high, raw_rows, 0)
+
+    def send_edges(e, buf):
+        for q in range(rows // 128):
+            span = slice(128 * q, 128 * q + 128)
+            turned = pack[span, 0:16].T
+            for m in range(5):
+                col_out[e, 0, m:m + 1, span] = turned[2 * m:2 * m + 1]
+                col_out[e, 1, m:m + 1, span] = turned[2 * m + 1:2 * m + 2]
+        for m in range(5):
+            src = fa if m == 4 else buf
+            if buf is None:
+                for side, row in ((0, rows - 1), (1, 0)):
+                    line = tally_v[row:row + 1, :].astype(F32) if m == 4 else temp_v[m, row:row + 1, :]
+                    row_out[e, side, m:m + 1, :] = line
+                continue
+            for h in range(2):
+                half = slice(128 * h, 128 * h + 128)
+                row_out[e, 0, m:m + 1, half] = src[m, h, PAD + rows - 1:PAD + rows, :]
+                row_out[e, 1, m:m + 1, half] = src[m, h, PAD:PAD + 1, :]
+        to_east = pltpu.make_async_remote_copy(
+            col_out.at[e, 0], col_in.at[e, 0], col_ss.at[e, 0], col_rs.at[e, 0], (d, y, east), MESH
+        )
+        to_west = pltpu.make_async_remote_copy(
+            col_out.at[e, 1], col_in.at[e, 1], col_ss.at[e, 1], col_rs.at[e, 1], (d, y, west), MESH
+        )
+        to_east.start()
+        to_west.start()
+
+        @pl.when(y < last)
+        def _():
+            pltpu.make_async_remote_copy(
+                row_out.at[e, 0], row_in.at[e, 1], row_ss.at[e, 0], row_rs.at[e, 1], (d, y + 1, b), MESH
+            ).start()
+
+        @pl.when(y == last)
+        def _():
+            pltpu.make_async_remote_copy(
+                row_out.at[e, 0], row_in.at[e, 0], row_ss.at[e, 0], row_rs.at[e, 0], (d, y, mirror), MESH
+            ).start()
+
+        @pl.when(y > 0)
+        def _():
+            pltpu.make_async_remote_copy(
+                row_out.at[e, 1], row_in.at[e, 0], row_ss.at[e, 1], row_rs.at[e, 0], (d, y - 1, b), MESH
+            ).start()
+
+        return to_east, to_west
+
     inner = jnp.logical_and(y > 0, y < last)
 
     @pl.when(inner)
@@ -184,6 +253,7 @@
         )
         copy.start()
         th_copies.append(copy)
+    edges = send_edges(0, None)
     tg_copies = []
     for j in range(1, nx):
         c = lax.rem(b + j, nx)
@@ -210,17 +280,8 @@
         prm[l, 6] = jnp.full((8, 128), thick[l] / full_norm, F32)
         top = top + thick[l]
 
-    def pack_edges(edges):
-        wide = lanes(edges[0].shape)
-        packed = jnp.zeros(edges[0].shape, F32)
-        for m, edge in enumerate(edges):
-            packed = jnp.where((wide >> 1) == m, pltpu.roll(edge, 2 * m + 1, 1), packed)
-        return packed
-
     def heat_rows(r, carry):
         base = pl.multiple_of(r * tall, tall)
-        first = masks(tall)[1]
-        fields = []
         for h in range(2):
             here = (pl.ds(base, tall), slice(128 * h, 128 * h + 128))
             tally = tally_v[here]
@@ -235,58 +296,22 @@
                     sums[k] = term if l == 0 else sums[k] + term
             for k in range(4):
                 fa[k, h, pl.ds(base + PAD, tall), :] = sums[k]
-            sums.append(fa[4, h, pl.ds(base + PAD, tall), :])
-            fields.append(sums)
-        pack[pl.ds(base, tall), :] = pack_edges(
-            [jnp.where(first, fields[0][m], fields[1][m]) for m in range(5)]
-        )
         return carry
 
-    for q in range(chunks):
-        temp_copies[q].wait()
-        lax.fori_loop(q * crow // tall, (q + 1) * crow // tall, heat_rows, 0)
-
-    def send_edges(e, buf):
-        for q in range(rows // 128):
-            span = slice(128 * q, 128 * q + 128)
-            turned = pack[span, 0:16].T
-            for m in range(5):
-                col_out[e, 0, m:m + 1, span] = turned[2 * m:2 * m + 1]
-                col_out[e, 1, m:m + 1, span] = turned[2 * m + 1:2 * m + 2]
-        for m in range(5):
-            src = fa if m == 4 else buf
-            for h in range(2):
-                half = slice(128 * h, 128 * h + 128)
-                row_out[e, 0, m:m + 1, half] = src[m, h, PAD + rows - 1:PAD + rows, :]
-                row_out[e, 1, m:m + 1, half] = src[m, h, PAD:PAD + 1, :]
-        to_east = pltpu.make_async_remote_copy(
-            col_out.at[e, 0], col_in.at[e, 0], col_ss.at[e, 0], col_rs.at[e, 0], (d, y, east), MESH
-        )
-        to_west = pltpu.make_async_remote_copy(
-            col_out.at[e, 1], col_in.at[e, 1], col_ss.at[e, 1], col_rs.at[e, 1], (d, y, west), MESH
-        )
-        to_east.start()
-        to_west.start()
-
-        @pl.when(y < last)
-        def _():
-            pltpu.make_async_remote_copy(
-                row_out.at[e, 0], row_in.at[e, 1], row_ss.at[e, 0], row_rs.at[e, 1], (d, y + 1, b), MESH
-            ).start()
-
-        @pl.when(y == last)
-        def _():
-            pltpu.make_async_remote_copy(
-                row_out.at[e, 0], row_in.at[e, 0], row_ss.at[e, 0], row_rs.at[e, 0], (d, y, mirror), MESH
-            ).start()
-
-        @pl.when(y > 0)
-        def _():
-            pltpu.make_async_remote_copy(
-                row_out.at[e, 1], row_in.at[e, 0], row_ss.at[e, 1], row_rs.at[e, 0], (d, y - 1, b), MESH
-            ).start()
-
-        return to_east, to_west
+    lax.fori_loop(0, rows // tall, heat_rows, 0)
+
+    def edge_fields(raw):
+        tally = raw[4]
+        sums = [None] * 4
+        for l in range(nl):
+            par = [prm[l, n, 0:1, 0:1] for n in range(7)]
+            t = raw[l]
+            heat = par[0] + (t + par[1]) / (par[2] + t * (therm_one + therm_two * t))
+            heat = jnp.where((d * nl + l).astype(F32) < tally, heat, 0.0)
+            for k in range(4):
+                term = par[3 + k] * heat
+                sums[k] = term if l == 0 else sums[k] + term
+        return sums + [jnp.where(tally > 0.0, 1.0, 0.0)]
 
     def receive_edges(e, copies):
         for copy in copies:
@@ -313,9 +338,18 @@
                 row_in[e, 0], flip, precision=lax.Precision.HIGHEST, preferred_element_type=F32
             )
 
-        for m in range(5):
-            pint[2 * m:2 * m + 1, :] = col_in[e, 1, m:m + 1, :]
-            pint[2 * m + 1:2 * m + 2, :] = col_in[e, 0, m:m + 1, :]
+        if e == 0:
+            for side in range(2):
+                fields = edge_fields([col_in[e, side, m:m + 1, :] for m in range(5)])
+                for m in range(5):
+                    pint[2 * m + 1 - side:2 * m + 2 - side, :] = fields[m]
+                fields = edge_fields([row_in[e, side, m:m + 1, :] for m in range(5)])
+                for m in range(5):
+                    row_in[e, side, m:m + 1, :] = fields[m]
+        else:
+            for m in range(5):
+                pint[2 * m:2 * m + 1, :] = col_in[e, 1, m:m + 1, :]
+                pint[2 * m + 1:2 * m + 2, :] = col_in[e, 0, m:m + 1, :]
         for q in range(rows // 128):
             span = slice(128 * q, 128 * q + 128)
             pin[span, 0:16] = pint[:, span].T
@@ -363,7 +397,6 @@
             )
         return fixed, wet
 
-    edges = send_edges(0, fa)
     sweep(fa, fb)
     receive_edges(0, edges)
     fix_rows(0, fa, fb)

time: 26.3 us -> 24.9 us (0.947)
  Pallas kernels: 25.5 us -> 24.1 us
    pallas_call x1, Pallas kernels: 25.5 us -> 24.1 us  [per_device(): pl.pallas_call(functools.partial(kernel, nd, ny, nx, cap, unroll, parts),...]
where the time goes in v5:
time: 24.9 us; the launch traced here: 24.8 us
  Pallas kernels  24.1 us (97%)
  local copies, waits for them, and re-layouts  0.63 us (3%)
    pallas_call x1, Pallas kernels, per_device(): pl.pallas_call(functools.partial(kernel, nd, ny, nx, cap, unroll, parts),...  24.1 us
    unnamed x1, local copies, waits for them, and re-layouts  0.63 us

profile of v5, /device:TPU:0, one launch (start us, length us, event | category | flops | bytes accessed | tf_op | source)
XLA Modules:
  0.0 24.8 jit_solution(1548594117267471535)
XLA Ops:
  0.0 24.1 %shard_map.73 = f32[128,128]{1,0:T(8,128)S(1)} custom-call(f32[4]{0:T(128)} %span_h.1, s32[2,512]{1,0:T(2,128)} %bitcast.8, f32[4,512,256]{2,1,0:T(8,128)} %temp_h.1, s32[512,256]{1,0:T(8,128)} %tally_h.1, s32[2,512]{1,0:T(2,128)} %bitcast.9, bf16[2,8192,128]{2,1,0:T(8,128)(2,1)} %bitcast.6, f32[128,128]{1,0:T(8,128)} %bitcast.7), custom_call_target="tpu_custom_call" | custom-call | tf_op jit(solution)/shard_map/pallas_call | solution.py:560
  24.1 0.6 %copy.9 = f32[1,128,128]{2,1,0:T(8,128)} copy(f32[1,128,128]{2,1,0:T(8,128)S(1)} %bitcast.5) | data formatting | bytes 131072
